TPU v7x, 32 devices: a whole 2x2x4 slice. The times are simulated.
32 devices in a mesh: grp: 2 (over x), res: 16 (over z, y, core).
Axes of the slice: x: 2, y: 2, z: 4, core: 2. Of those that a mesh axis runs over, the one named last changes fastest.
Arguments:
- queries: bfloat16 [8192, 512], P(('grp', 'res')), parts along dimension 0, may hold values from -6 to 6
- query_points: bfloat16 [8192, 384], P(('grp', 'res')), parts along dimension 0, may hold values from -5 to 8
- keys: bfloat16 [8192, 512], P(('grp', 'res')), parts along dimension 0, may hold values from -6 to 6
- key_points: bfloat16 [8192, 384], P(('grp', 'res')), parts along dimension 0, may hold values from -6 to 6
- values: bfloat16 [8192, 512], P(('grp', 'res')), parts along dimension 0, may hold values from -6 to 6
- point_weights: float32 [16], replicated, may hold values from 0.3 to 3
- out_grad: bfloat16 [8192, 512], P(('grp', 'res')), parts along dimension 0, may hold values from -6 to 6
- fetch_block: int32 [32, 16], P(('grp', 'res')), parts along dimension 0, may hold values from 0 to 1
- key_owner: int32 [64, 16], P(('grp', 'res')), parts along dimension 0, may hold values from 0 to 15, as said below
- key_live: int32 [64, 16], P(('grp', 'res')), parts along dimension 0, may hold values from 0 to 1, as said below
Outputs:
- query_grad: float32 [8192, 512], P(('grp', 'res')), parts along dimension 0
- query_point_grad: float32 [8192, 384], P(('grp', 'res')), parts along dimension 0
- key_grad: float32 [8192, 512], P(('grp', 'res')), parts along dimension 0
- key_point_grad: float32 [8192, 384], P(('grp', 'res')), parts along dimension 0
- value_grad: float32 [8192, 512], P(('grp', 'res')), parts along dimension 0
There are 2 independent parts, one for each index of `grp`. A program takes and returns all parts, laid end to end along the dimension named above; an argument that names none is the same for every part. Nothing has to cross between parts.
Inputs may be any that keep to these rules, and one draw needn't show every extreme that they name: `key_owner`: the 16 entries of one query block name distinct devices. `key_live`: in each row the live slots come first; a row has 4 to 16 of them, and row 0 has all.
All inputs are finite; a program needn't handle non-finite values.
Results may differ from a plain program's by a relative error of at most 0.012.
The roundings to bfloat16 on the way count: a program that leaves them out, or rounds other values in their place, can miss the bound.
Values may be sent and summed in bfloat16 or wider, within the bound.
A program may use at most 192 MiB of HBM per device.

v0:
```python
import math

import jax
import jax.numpy as jnp
from jax import lax
from jax.sharding import PartitionSpec as P

BLOCK = 128


LOGIT_WEIGHT = math.sqrt(1.0 / 3.0)


def block_grads(query_block, query_pts, cot_block, gathered, live_cols, weights):
    row_count = query_block.shape[0]
    model_width = query_block.shape[1]
    head_count = weights.shape[0]
    head_dim = model_width // head_count
    points = query_pts.shape[1] // (3 * head_count)
    key_count = gathered.shape[0]
    key_part = gathered[:, :model_width].reshape(key_count, head_count, head_dim)
    value_part = gathered[:, model_width : 2 * model_width].reshape(key_count, head_count, head_dim)
    key_grid = gathered[:, 2 * model_width :].reshape(key_count, 3, head_count, points)
    query_heads = query_block.reshape(row_count, head_count, head_dim)
    cot_heads = cot_block.reshape(row_count, head_count, head_dim)
    query_grid = query_pts.reshape(row_count, 3, head_count, points)
    scalar_scale = LOGIT_WEIGHT / math.sqrt(head_dim)
    point_scale = LOGIT_WEIGHT * math.sqrt(2.0 / (9.0 * points)) * weights
    scores = jnp.einsum("bhc,mhc->hbm", query_heads, key_part, preferred_element_type=jnp.float32)
    crossed = jnp.einsum("bxhp,mxhp->hbm", query_grid, key_grid, preferred_element_type=jnp.float32)
    query_wide = query_grid.astype(jnp.float32)
    key_wide = key_grid.astype(jnp.float32)
    query_sq = jnp.sum(query_wide * query_wide, axis=(1, 3)).T
    key_sq = jnp.sum(key_wide * key_wide, axis=(1, 3)).T
    distance = query_sq[:, :, None] + key_sq[:, None, :] - 2.0 * crossed
    logits = scalar_scale * scores - 0.5 * point_scale[:, None, None] * distance
    logits = jnp.where(live_cols[None, None, :], logits, -jnp.inf)
    highest = jnp.max(logits, axis=2, keepdims=True)
    exponent = jnp.exp(logits - highest)
    softmax_weights = exponent / jnp.sum(exponent, axis=2, keepdims=True)
    probs_low = softmax_weights.astype(jnp.bfloat16)
    attended = jnp.einsum("hbm,mhc->bhc", probs_low, value_part, preferred_element_type=jnp.float32)
    delta_term = jnp.sum(cot_heads.astype(jnp.float32) * attended, axis=2).T
    prob_grad = jnp.einsum(
        "bhc,mhc->hbm", cot_heads, value_part, preferred_element_type=jnp.float32
    )
    score_grad = softmax_weights * (prob_grad - delta_term[:, :, None])
    score_low = score_grad.astype(jnp.bfloat16)
    query_grad = scalar_scale * jnp.einsum(
        "hbm,mhc->bhc", score_low, key_part, preferred_element_type=jnp.float32
    )
    row_total = jnp.sum(score_grad, axis=2).T
    point_pull = jnp.einsum(
        "hbm,mxhp->bxhp", score_low, key_grid, preferred_element_type=jnp.float32
    )
    query_point_grad = -point_scale[None, None, :, None] * (
        row_total[:, None, :, None] * query_wide - point_pull
    )
    key_grad = scalar_scale * jnp.einsum(
        "hbm,bhc->mhc", score_low, query_heads, preferred_element_type=jnp.float32
    )
    col_total = jnp.sum(score_grad, axis=1).T
    key_pull = jnp.einsum(
        "hbm,bxhp->mxhp", score_low, query_grid, preferred_element_type=jnp.float32
    )
    key_point_grad = point_scale[None, None, :, None] * (
        key_pull - col_total[:, None, :, None] * key_wide
    )
    value_grad = jnp.einsum(
        "hbm,bhc->mhc", probs_low, cot_heads, preferred_element_type=jnp.float32
    )
    slot_terms = jnp.concatenate(
        [
            key_grad.reshape(key_count, model_width),
            value_grad.reshape(key_count, model_width),
            key_point_grad.reshape(key_count, -1),
        ],
        axis=1,
    )
    return (
        query_grad.reshape(row_count, model_width),
        query_point_grad.reshape(row_count, -1),
        slot_terms,
    )


def local(
    queries,
    query_points,
    keys,
    key_points,
    values,
    point_weights,
    out_grad,
    fetch_block,
    key_owner,
    key_live,
):
    owners = lax.axis_size("res")
    row_count = queries.shape[0]
    block_count = row_count // BLOCK
    model_width = queries.shape[1]
    point_width = query_points.shape[1]
    request_table = lax.all_gather(fetch_block, "res", axis=0, tiled=True)
    wanted = lax.dynamic_slice_in_dim(request_table, lax.axis_index("res"), 1, 1)[:, 0]
    packed = jnp.concatenate([keys, values, key_points], axis=1).reshape(block_count, BLOCK, -1)
    feature_count = packed.shape[2]
    outgoing = jnp.take(packed, wanted, axis=0)
    fetched = lax.all_to_all(outgoing, "res", split_axis=0, concat_axis=0, tiled=True)
    owner_ids = jnp.arange(owners, dtype=jnp.int32)

    def per_block(running, inputs):
        query_block, query_pts, cot_block, owner_row, live_row = inputs
        gathered = jnp.take(fetched, owner_row, axis=0).reshape(-1, feature_count)
        live_cols = jnp.repeat(live_row > 0, BLOCK)
        query_grad, point_grad, slot_terms = block_grads(
            query_block, query_pts, cot_block, gathered, live_cols, point_weights
        )
        running = running.at[owner_row].add(slot_terms.reshape(-1, BLOCK, feature_count))
        return (running, (query_grad, point_grad))

    inputs = (
        queries.reshape(block_count, BLOCK, model_width),
        query_points.reshape(block_count, BLOCK, point_width),
        out_grad.reshape(block_count, BLOCK, model_width),
        key_owner,
        key_live,
    )
    slot_sums, (query_grads, point_grads) = lax.scan(
        per_block, jnp.zeros((owners, BLOCK, feature_count), jnp.float32), inputs
    )
    rounded = slot_sums.astype(jnp.bfloat16)
    targets = owner_ids * block_count + fetch_block[0]
    block_ids = jnp.arange(row_count * lax.axis_size("res") // BLOCK, dtype=jnp.int32)
    picker = (block_ids[:, None] == targets[None, :]).astype(jnp.bfloat16)
    summed = lax.psum_scatter(
        jnp.einsum("bo,otf->btf", picker, rounded, preferred_element_type=jnp.float32)
        .reshape(row_count * lax.axis_size("res"), feature_count)
        .astype(jnp.bfloat16),
        "res",
        scatter_dimension=0,
        tiled=True,
    ).astype(jnp.float32)
    return (
        query_grads.reshape(row_count, model_width),
        point_grads.reshape(row_count, point_width),
        summed[:, :model_width],
        summed[:, 2 * model_width :],
        summed[:, model_width : 2 * model_width],
    )


def solution(mesh):
    return jax.shard_map(
        local,
        mesh=mesh,
        in_specs=(
            P(("grp", "res"), None),
            P(("grp", "res"), None),
            P(("grp", "res"), None),
            P(("grp", "res"), None),
            P(("grp", "res"), None),
            P(),
            P(("grp", "res"), None),
            P(("grp", "res"), None),
            P(("grp", "res"), None),
            P(("grp", "res"), None),
        ),
        out_specs=(
            P(("grp", "res"), None),
            P(("grp", "res"), None),
            P(("grp", "res"), None),
            P(("grp", "res"), None),
            P(("grp", "res"), None),
        ),
        check_vma=False,
    )
```

profile of v0, /device:TPU:0, one launch (start us, length us, event | category | flops | bytes accessed | tf_op | source)
XLA Modules:
  0.0 627.0 jit_solution(8287984148876067285)
XLA Ops:
  7.2 23.2 %all-gather = s32[16,1,16]{2,1,0:T(1,128)S(1)} all-gather(s32[1,1,16]{2,1,0:T(1,128)} %bitcast.254), channel_id=1, replica_groups=mesh['grp'=2,'res'=16] {'res'}, dimensions={0}, use_global_device_ids=true | all-gather | bytes 1088 | tf_op jit(solution)/shard_map/all_gather | solution.py:104
  35.7 5.7 broadcast_select_fusion.1
  46.8 104.4 %all-to-all-done = bf16[16,128,1408]{2,1,0:T(8,128)(2,1)} async-done(((bf16[16,128,1408]{2,1,0:T(8,128)(2,1)}), bf16[16,128,1408]{2,1,0:T(8,128)(2,1)}, u32[]{:S(2)}, u32[]{:S(2)}) %all-to-all-start) | async-done | bytes 5767200 | tf_op jit(solution)/shard_map/all_to_all | solution.py:109
  151.2 5.5 broadcast_in_dim.89
  156.7 288.8 %while.16 = (s32[]{:T(128)}, f32[16,128,1408]{2,1,0:T(8,128)}, f32[2,128,512]{2,1,0:T(8,128)}, f32[2,128,384]{2,1,0:T(8,128)}, s32[2,16]{1,0:T(2,128)S(1)}, /*in...) while((s32[]{:T(128)}, f32[16,128,1408]{2,1,0:T(8,128)}, ...), condition=%wide.region_9.10_spmd, body=%wide.region_0.9_spmd.sunk | while | flops 2304521472 | bytes 427316480 | solution.py:129
  159.3 6.3 %gather_fusion = bf16[16,128,1408]{2,1,0:T(8,128)(2,1)} fusion(bf16[16,128,1408]{2,1,0:T(8,128)(2,1)} %get-tuple-element.339, s32[1024]{0:T(1024)S(1)} %pad_clamp_fusion.3), kind=kCustom, calls=%fused_computation.clone.1 | custom fusion | bytes 11534400 | tf_op jit(solution)/shard_map/while/body/eval_jaxpr/jit(_take)/gather | solution.py:114
  165.6 8.2 %copy.126 = bf16[2048,1408]{0,1:T(8,128)(2,1)} copy(bf16[2048,1408]{1,0:T(8,128)(2,1)} %bitcast.224) | data formatting | bytes 11534336 | tf_op jit(solution)/shard_map/while/body/eval_jaxpr/jit(_take)/gather | solution.py:114
  180.1 8.1 %fusion.113 = f32[16,128,2048,1]{2,1,0,3:T(8,128)} fusion(bf16[128,3,16,8]{0,3,2,1:T(8,128)(2,1)S(1)} %bitcast.234, bf16[2048,3,16,8]{0,3,2,1:T(8,128)(2,1)S(1)} %bitcast.219), kind=kOutput, calls=%fused_computation.72.clone.1 | convolution fusion | flops 201326592 | bytes 18448384 | tf_op jit(solution)/shard_map/while/body/eval_jaxpr/bxhp,mxhp->hbm/dot_general | solution.py:30
  188.2 15.0 %fusion.117 = (f32[16,128]{1,0:T(8,128)S(1)}, f32[16,128,2048]{2,1,0:T(8,128)}) fusion(f32[16,128,2048,1]{2,1,0,3:T(8,128)} %fusion.113, f32[16,2048]{1,0:T(8,128)S(1)} %bitcast.247, f32[16,128]{1,0:T(8,128)S(1)} %bitcast.252, f32[16]{0:T(128)S(1)} %get-tuple-element.297, pred[2048]{0:T(1024)(128)(4,1)S(1)} %broadcast_bitcast_fusion.5, ...), kind=kOutput, calls=%fused_computation.70.clone.1 | convolution fusion | flops 306186240 | bytes 35932224 | tf_op jit(solution)/shard_map/while/body/eval_jaxpr/sub | solution.py:39
  203.2 7.3 %fusion.118 = bf16[16,128,2048]{2,1,0:T(8,128)(2,1)S(1)} fusion(f32[16,128,2048]{2,1,0:T(8,128)} %get-tuple-element.300, f32[16,128]{1,0:T(8,128)S(1)} %get-tuple-element.301), kind=kLoop, calls=%fused_computation.17.clone.1 | loop fusion | flops 8388608 | bytes 25174016 | tf_op jit(solution)/shard_map/while/body/eval_jaxpr/convert_element_type | solution.py:41
  217.5 5.3 copy.134
  222.9 8.9 %fusion.120 = (f32[16,128]{1,0:T(8,128)S(1)}, f32[16,2048]{1,0:T(8,128)S(1)}, bf16[16,128,2048]{2,1,0:T(8,128)(2,1)S(1)}) fusion(f32[16,128]{1,0:T(8,128)S(1)} %bitcast.251, bf16[128,16,32]{0,2,1:T(8,128)(2,1)S(1)} %bitcast.241, bf16[2048,16,32]{0,2,1:T(8,128)(2,1)} %bitcast.231, f32[16,128,2048]{2,1,0:T(8,128)} %get-tuple-element.300, ...), kind=kOutput, calls=%fused_computation.68.clone.1 | convolution fusion | flops 293566464 | bytes 27549696 | tf_op jit(solution)/shard_map/while/body/eval_jaxpr/bhc,mhc->hbm/dot_general | solution.py:44
  238.0 5.7 fusion.123
  245.3 6.8 %fusion.121 = f32[2048,3,16,8]{0,3,1,2:T(8,128)} fusion(bf16[16,128,2048]{2,1,0:T(8,128)(2,1)} %copy-done, f32[2048,16]{0,1:T(8,128)S(1)} %bitcast.242, f32[16]{0:T(128)S(1)} %get-tuple-element.305, bf16[2048,3,16,8]{0,3,2,1:T(8,128)(2,1)S(1)} %bitcast.221, bf16[128,3,16,8]{0,3,2,1:T(8,128)(2,1)S(1)} %bitcast.236), kind=kOutput, calls=%fused_computation.24.clone.1 | convolution fusion | flops 204472320 | bytes 13336640 | tf_op jit(solution)/shard_map/while/body/eval_jaxpr/hbm,bxhp->mxhp/dot_general | solution.py:63
  256.1 5.5 copy.136
  264.9 8.8 %pad_maximum_fusion.3 = f32[16,128,1408]{2,1,0:T(8,128)} fusion(f32[16,128,384]{2,1,0:T(8,128)} %copy.132, f32[16,128,512]{2,1,0:T(8,128)} %copy.134, f32[16,128,512]{2,1,0:T(8,128)} %copy.136), kind=kLoop, calls=%fused_computation.11.clone.1 | loop fusion | flops 5767168 | bytes 23068672 | tf_op jit(solution)/shard_map/while/body/eval_jaxpr/concatenate | solution.py:72
  273.6 27.6 %scatter_fusion = f32[16,128,1408]{2,1,0:T(8,128)} fusion(f32[16,128,1408]{2,1,0:T(8,128)} %get-tuple-element.321, s32[16]{0:T(128)S(1)} %fusion.111, f32[16,128,1408]{2,1,0:T(8,128)} %pad_maximum_fusion.3), kind=kCustom, calls=%fused_computation.2.clone.1 | custom fusion | flops 2883584 | bytes 34603072 | tf_op jit(solution)/shard_map/while/body/eval_jaxpr/scatter-add | solution.py:119
  303.7 6.3 %gather_fusion = bf16[16,128,1408]{2,1,0:T(8,128)(2,1)} fusion(bf16[16,128,1408]{2,1,0:T(8,128)(2,1)} %get-tuple-element.339, s32[1024]{0:T(1024)S(1)} %pad_clamp_fusion.3), kind=kCustom, calls=%fused_computation.clone.1 | custom fusion | bytes 11534400 | tf_op jit(solution)/shard_map/while/body/eval_jaxpr/jit(_take)/gather | solution.py:114
  310.0 8.2 %copy.126 = bf16[2048,1408]{0,1:T(8,128)(2,1)} copy(bf16[2048,1408]{1,0:T(8,128)(2,1)} %bitcast.224) | data formatting | bytes 11534336 | tf_op jit(solution)/shard_map/while/body/eval_jaxpr/jit(_take)/gather | solution.py:114
  324.5 8.1 %fusion.113 = f32[16,128,2048,1]{2,1,0,3:T(8,128)} fusion(bf16[128,3,16,8]{0,3,2,1:T(8,128)(2,1)S(1)} %bitcast.234, bf16[2048,3,16,8]{0,3,2,1:T(8,128)(2,1)S(1)} %bitcast.219), kind=kOutput, calls=%fused_computation.72.clone.1 | convolution fusion | flops 201326592 | bytes 18448384 | tf_op jit(solution)/shard_map/while/body/eval_jaxpr/bxhp,mxhp->hbm/dot_general | solution.py:30
  332.6 15.0 %fusion.117 = (f32[16,128]{1,0:T(8,128)S(1)}, f32[16,128,2048]{2,1,0:T(8,128)}) fusion(f32[16,128,2048,1]{2,1,0,3:T(8,128)} %fusion.113, f32[16,2048]{1,0:T(8,128)S(1)} %bitcast.247, f32[16,128]{1,0:T(8,128)S(1)} %bitcast.252, f32[16]{0:T(128)S(1)} %get-tuple-element.297, pred[2048]{0:T(1024)(128)(4,1)S(1)} %broadcast_bitcast_fusion.5, ...), kind=kOutput, calls=%fused_computation.70.clone.1 | convolution fusion | flops 306186240 | bytes 35932224 | tf_op jit(solution)/shard_map/while/body/eval_jaxpr/sub | solution.py:39
  347.6 7.3 %fusion.118 = bf16[16,128,2048]{2,1,0:T(8,128)(2,1)S(1)} fusion(f32[16,128,2048]{2,1,0:T(8,128)} %get-tuple-element.300, f32[16,128]{1,0:T(8,128)S(1)} %get-tuple-element.301), kind=kLoop, calls=%fused_computation.17.clone.1 | loop fusion | flops 8388608 | bytes 25174016 | tf_op jit(solution)/shard_map/while/body/eval_jaxpr/convert_element_type | solution.py:41
  361.9 5.3 copy.134
  367.2 8.9 %fusion.120 = (f32[16,128]{1,0:T(8,128)S(1)}, f32[16,2048]{1,0:T(8,128)S(1)}, bf16[16,128,2048]{2,1,0:T(8,128)(2,1)S(1)}) fusion(f32[16,128]{1,0:T(8,128)S(1)} %bitcast.251, bf16[128,16,32]{0,2,1:T(8,128)(2,1)S(1)} %bitcast.241, bf16[2048,16,32]{0,2,1:T(8,128)(2,1)} %bitcast.231, f32[16,128,2048]{2,1,0:T(8,128)} %get-tuple-element.300, ...), kind=kOutput, calls=%fused_computation.68.clone.1 | convolution fusion | flops 293566464 | bytes 27549696 | tf_op jit(solution)/shard_map/while/body/eval_jaxpr/bhc,mhc->hbm/dot_general | solution.py:44
  382.4 5.7 fusion.123
  389.7 6.8 %fusion.121 = f32[2048,3,16,8]{0,3,1,2:T(8,128)} fusion(bf16[16,128,2048]{2,1,0:T(8,128)(2,1)} %copy-done, f32[2048,16]{0,1:T(8,128)S(1)} %bitcast.242, f32[16]{0:T(128)S(1)} %get-tuple-element.305, bf16[2048,3,16,8]{0,3,2,1:T(8,128)(2,1)S(1)} %bitcast.221, bf16[128,3,16,8]{0,3,2,1:T(8,128)(2,1)S(1)} %bitcast.236), kind=kOutput, calls=%fused_computation.24.clone.1 | convolution fusion | flops 204472320 | bytes 13336640 | tf_op jit(solution)/shard_map/while/body/eval_jaxpr/hbm,bxhp->mxhp/dot_general | solution.py:63
  400.5 5.5 copy.136
  409.2 8.8 %pad_maximum_fusion.3 = f32[16,128,1408]{2,1,0:T(8,128)} fusion(f32[16,128,384]{2,1,0:T(8,128)} %copy.132, f32[16,128,512]{2,1,0:T(8,128)} %copy.134, f32[16,128,512]{2,1,0:T(8,128)} %copy.136), kind=kLoop, calls=%fused_computation.11.clone.1 | loop fusion | flops 5767168 | bytes 23068672 | tf_op jit(solution)/shard_map/while/body/eval_jaxpr/concatenate | solution.py:72
  418.0 27.5 %scatter_fusion = f32[16,128,1408]{2,1,0:T(8,128)} fusion(f32[16,128,1408]{2,1,0:T(8,128)} %get-tuple-element.321, s32[16]{0:T(128)S(1)} %fusion.111, f32[16,128,1408]{2,1,0:T(8,128)} %pad_maximum_fusion.3), kind=kCustom, calls=%fused_computation.2.clone.1 | custom fusion | flops 2883584 | bytes 34603072 | tf_op jit(solution)/shard_map/while/body/eval_jaxpr/scatter-add | solution.py:119
  450.6 7.3 %convolution_convert_fusion = bf16[32,128,1408]{2,0,1:T(8,128)(2,1)S(1)} fusion(bf16[16,128,1408]{2,1,0:T(8,128)(2,1)S(1)} %convert_element_type.47, s32[16]{0:T(128)S(1)} %copy-done.6), kind=kOutput, calls=%fused_computation.55 | convolution fusion | flops 190317056 | bytes 17301568 | tf_op jit(solution)/shard_map/bo,otf->btf/dot_general | solution.py:137
  457.9 10.7 %copy.71 = bf16[32,128,1408]{2,1,0:T(8,128)(2,1)} copy(bf16[32,128,1408]{2,0,1:T(8,128)(2,1)S(1)} %convolution_convert_fusion) | data formatting | bytes 23068672 | tf_op jit(solution)/shard_map/convert_element_type | solution.py:139
  468.6 147.7 %reduce-scatter.2.cloned.1.call-done = bf16[256,1408]{1,0:T(8,128)(2,1)} async-done(((bf16[4096,1408]{1,0:T(8,128)(2,1)}), bf16[256,1408]{1,0:T(8,128)(2,1)}) %reduce-scatter.2.cloned.1.call-update) | async-done | bytes 720912 | tf_op jit(solution)/shard_map/reduce_scatter | solution.py:136
  (115 shorter events, 81.3 us)
Async XLA Ops:
  41.4 4.8 copy-start.7
  41.4 109.7 %all-to-all-start = ((bf16[16,128,1408]{2,1,0:T(8,128)(2,1)}), bf16[16,128,1408]{2,1,0:T(8,128)(2,1)}, u32[]{:S(2)}, u32[]{:S(2)}) async-start(bf16[16,128,1408]{2,1,0:T(8,128)(2,1)} %broadcast_select_fusion.1), calls=%async_computation | async-start | bytes 11534336 | tf_op jit(solution)/shard_map/all_to_all | solution.py:109
  46.2 570.2 %reduce-scatter.2.cloned.1.call-start = ((), (), s32[]{:S(2)}) async-start(), calls=%async_computation.2 | async-start | bytes 12255232 | tf_op jit(solution)/shard_map/reduce_scatter | solution.py:136
  151.2 5.5 copy-start.4
  151.2 5.5 copy-start.5
  151.2 5.5 copy-start.8
  151.2 5.5 copy-start.9
  203.2 7.3 %copy-start.3 = (bf16[2048,512]{0,1:T(8,128)(2,1)S(1)}, bf16[2048,512]{0,1:T(8,128)(2,1)}, u32[]{:S(2)}) copy-start(bf16[2048,512]{0,1:T(8,128)(2,1)} %get-tuple-element.296) | copy-start | bytes 6291460 | tf_op jit(solution)/shard_map/while
  222.8 12.1 %copy-start.2 = (bf16[2048,512]{0,1:T(8,128)(2,1)S(1)}, bf16[2048,512]{0,1:T(8,128)(2,1)}, u32[]{:S(2)}) copy-start(bf16[2048,512]{0,1:T(8,128)(2,1)} %get-tuple-element.299) | copy-start | bytes 6291460 | tf_op jit(solution)/shard_map/while
  231.8 3.2 copy-start
  244.6 7.5 %slice-start = ((s8[8388608]{0:T(1024)(128)(4,1)}), s8[4194304]{0:T(1024)(128)(4,1)S(1)}, s32[]{:S(2)}) async-start(s8[8388608]{0:T(1024)(128)(4,1)} %bitcast.216), calls=%async_computation.3 | async-start | bytes 8388608 | tf_op jit(solution)/shard_map/while
  245.3 6.8 %slice-start.1 = ((s8[8388608]{0:T(1024)(128)(4,1)}), s8[4194304]{0:T(1024)(128)(4,1)S(1)}, s32[]{:S(2)}) async-start(s8[8388608]{0:T(1024)(128)(4,1)} %bitcast.216), calls=%async_computation.4 | async-start | bytes 8388608 | tf_op jit(solution)/shard_map/while
  256.1 5.5 copy-start.1
  347.6 7.3 %copy-start.3 = (bf16[2048,512]{0,1:T(8,128)(2,1)S(1)}, bf16[2048,512]{0,1:T(8,128)(2,1)}, u32[]{:S(2)}) copy-start(bf16[2048,512]{0,1:T(8,128)(2,1)} %get-tuple-element.296) | copy-start | bytes 6291460 | tf_op jit(solution)/shard_map/while
  367.2 12.1 %copy-start.2 = (bf16[2048,512]{0,1:T(8,128)(2,1)S(1)}, bf16[2048,512]{0,1:T(8,128)(2,1)}, u32[]{:S(2)}) copy-start(bf16[2048,512]{0,1:T(8,128)(2,1)} %get-tuple-element.299) | copy-start | bytes 6291460 | tf_op jit(solution)/shard_map/while
  376.1 3.2 copy-start
  388.9 7.5 %slice-start = ((s8[8388608]{0:T(1024)(128)(4,1)}), s8[4194304]{0:T(1024)(128)(4,1)S(1)}, s32[]{:S(2)}) async-start(s8[8388608]{0:T(1024)(128)(4,1)} %bitcast.216), calls=%async_computation.3 | async-start | bytes 8388608 | tf_op jit(solution)/shard_map/while
  389.6 6.8 %slice-start.1 = ((s8[8388608]{0:T(1024)(128)(4,1)}), s8[4194304]{0:T(1024)(128)(4,1)S(1)}, s32[]{:S(2)}) async-start(s8[8388608]{0:T(1024)(128)(4,1)} %bitcast.216), calls=%async_computation.4 | async-start | bytes 8388608 | tf_op jit(solution)/shard_map/while
  400.5 5.5 copy-start.1
  445.5 5.1 copy-start.6
Sparse Core Ops, SparseCore 0:
  468.7 147.5 reduce-scatter.1
where the time goes:
time: 629 us; the launch traced here: 627 us
  waiting for transfers between devices  252 us (40%)
  matrix products  113 us (18%)
  local copies, waits for them, and re-layouts  112 us (18%)
  other arithmetic  107 us (17%)
  blocking collectives  23.2 us (4%)
  between operations  14.1 us (2%)
    reduce_scatter x1, waiting for transfers between devices, local(): lax.psum_scatter(jnp.einsum('bo,otf->btf', picker, rounded, preferred_ele...  148 us
    all_to_all x1, waiting for transfers between devices, local(): lax.all_to_all(outgoing, 'res', split_axis=0, concat_axis=0, tiled=True)  104 us
    scatter-add x2, other arithmetic, per_block(): running.at[owner_row].add(slot_terms.reshape(-1, BLOCK, feature_count))  55.1 us
    sub x2, matrix products, block_grads(): exponent = jnp.exp(logits - highest)  30 us
    gather x4, local copies, waits for them, and re-layouts, per_block(): gathered = jnp.take(fetched, owner_row, axis=0).reshape(-1, feature_count)  29 us
    concatenate x6, local copies, waits for them, and re-layouts, block_grads(): jnp.concatenate([key_grad.reshape(key_count, model_width), value_grad.res...  26.3 us
    all_gather x1, blocking collectives, local(): request_table = lax.all_gather(fetch_block, 'res', axis=0, tiled=True)  23.2 us
    while x30, local copies, waits for them, and re-layouts  19.2 us
  transfers between devices with their start and end apart: 2, of which 2 were waited for; matrix products, arithmetic and copies ran while one was open for 0% of the time, Pallas kernels for 0%

commit v1 on v0

v1 whole, which is shorter than its diff:
```python
import functools
import math

import jax
import jax.numpy as jnp
from jax import lax
from jax.experimental import pallas as pl
from jax.experimental.pallas import tpu as pltpu
from jax.sharding import PartitionSpec as P

BLOCK = 128
LOGIT_WEIGHT = math.sqrt(1.0 / 3.0)
HEAD_COLS = 64
QUAD = 4
CHUNK = 2 * BLOCK
F32 = jnp.float32
BF16 = jnp.bfloat16


def dot(a, b):
    return jnp.dot(a, b, preferred_element_type=F32)


def fold(x, op):
    return op(x.reshape(x.shape[0] // 8, 8, x.shape[1]), axis=0)


def attention_kernel(
    head_dim, point_cols, kx_ref, v_ref, qhi_ref, qlo_ref, qraw_ref, cot_ref, cott_ref, qt_ref,
    bias_ref, colscale_ref, colpoint_ref, rowscale_ref, rowpoint_ref,
    kterm_ref, vterm_ref, qgrad_ref, s_ref, d_ref,
):
    keys = kx_ref.shape[0]
    cols = qhi_ref.shape[1]
    chunks = keys // CHUNK
    zeros = jnp.zeros((HEAD_COLS, cols), BF16)

    def score_weights(h):
        rows = slice(h * HEAD_COLS, (h + 1) * HEAD_COLS)
        hi, lo = qhi_ref[rows, :], qlo_ref[rows, :]
        parts = [hi, zeros, lo, zeros] if h % 2 == 0 else [zeros, hi, zeros, lo]
        return jnp.concatenate(parts, axis=0)

    def cot_weights(h):
        row = lax.broadcasted_iota(jnp.int32, (QUAD * head_dim, cols), 0)
        keep = (row >= h * head_dim) & (row < (h + 1) * head_dim)
        return jnp.where(keep, cott_ref[...], jnp.zeros((), BF16))

    qw = [score_weights(h) for h in range(QUAD)]
    ow = [cot_weights(h) for h in range(QUAD)]

    def scores(i, highest):
        rows = pl.ds(pl.multiple_of(i * CHUNK, CHUNK), CHUNK)
        low = bias_ref[pl.ds(i * 2, 1), :]
        high = bias_ref[pl.ds(i * 2 + 1, 1), :]
        vals = v_ref[rows, :]
        out = []
        for h in range(QUAD):
            pair = kx_ref[rows, (h // 2) * 128 : (h // 2 + 1) * 128]
            s = dot(jnp.concatenate([pair, pair], axis=1), qw[h])
            s = jnp.concatenate([s[:BLOCK] + low, s[BLOCK:] + high], axis=0)
            s_ref[h, rows, :] = s
            out.append(jnp.maximum(highest[h], fold(s, jnp.max)))
            d_ref[h, rows, :] = dot(vals, ow[h])
        return tuple(out)

    highest = lax.fori_loop(
        0, chunks, scores, tuple(jnp.full((8, cols), -jnp.inf, F32) for _ in range(QUAD))
    )
    highest = [jnp.max(x, axis=0, keepdims=True) for x in highest]

    def exps(i, total):
        rows = pl.ds(pl.multiple_of(i * CHUNK, CHUNK), CHUNK)
        out = []
        for h in range(QUAD):
            e = jnp.exp(s_ref[h, rows, :] - highest[h])
            s_ref[h, rows, :] = e
            out.append(total[h] + fold(e, jnp.sum))
        return tuple(out)

    zero8 = tuple(jnp.zeros((8, cols), F32) for _ in range(QUAD))
    total = lax.fori_loop(0, chunks, exps, zero8)
    inverse = [1.0 / jnp.sum(x, axis=0, keepdims=True) for x in total]

    def deltas(i, delta):
        rows = pl.ds(pl.multiple_of(i * CHUNK, CHUNK), CHUNK)
        out = []
        for h in range(QUAD):
            p = s_ref[h, rows, :] * inverse[h]
            low = p.astype(BF16).astype(F32)
            out.append(delta[h] + fold(low * d_ref[h, rows, :], jnp.sum))
        return tuple(out)

    delta = lax.fori_loop(0, chunks, deltas, zero8)
    delta = [jnp.sum(x, axis=0, keepdims=True) for x in delta]

    lane = lax.broadcasted_iota(jnp.int32, (cols, 128), 1)
    qk = []
    ok = []
    for h in range(QUAD):
        pair = qraw_ref[:, (h // 2) * 128 : (h // 2 + 1) * 128]
        qk.append(jnp.where(lane // HEAD_COLS == h % 2, pair, jnp.zeros((), BF16)))
        ok.append(jnp.where(lane // head_dim == h, cot_ref[...], jnp.zeros((), BF16)))
    half = lax.broadcasted_iota(jnp.int32, (CHUNK, 128), 1) < HEAD_COLS

    def grads(i, carry):
        row_total, pulls = carry
        rows = pl.ds(pl.multiple_of(i * CHUNK, CHUNK), CHUNK)
        new_total, new_pulls = [], []
        vterm = None
        for g in range(QUAD // 2):
            pair = kx_ref[rows, g * 128 : (g + 1) * 128]
            kterm = None
            col_totals = []
            for h in (2 * g, 2 * g + 1):
                p = s_ref[h, rows, :] * inverse[h]
                p_low = p.astype(BF16)
                ds = p * (d_ref[h, rows, :] - delta[h])
                ds_low = ds.astype(BF16)
                new_total.append(row_total[h] + fold(ds, jnp.sum))
                col_totals.append(jnp.sum(ds, axis=1, keepdims=True))
                kt = dot(ds_low, qk[h])
                kterm = kt if kterm is None else kterm + kt
                vt = dot(p_low, ok[h])
                vterm = vt if vterm is None else vterm + vt
                pull = lax.dot_general(
                    pair, ds_low, (((0,), (0,)), ((), ())), preferred_element_type=F32
                )
                off = (h % 2) * HEAD_COLS
                new_pulls.append(pulls[h] + pull[off : off + HEAD_COLS])
            sums = jnp.where(half, col_totals[0], col_totals[1])
            span = slice(g * 128, (g + 1) * 128)
            kterm = colscale_ref[:, span] * kterm - colpoint_ref[:, span] * sums * pair.astype(F32)
            kterm_ref[rows, span] = kterm.astype(BF16)
        vterm_ref[rows, :] = vterm.astype(BF16)
        return tuple(new_total), tuple(new_pulls)

    pull0 = tuple(jnp.zeros((HEAD_COLS, cols), F32) for _ in range(QUAD))
    row_total, pulls = lax.fori_loop(0, chunks, grads, (zero8, pull0))
    for h in range(QUAD):
        rows = slice(h * HEAD_COLS, (h + 1) * HEAD_COLS)
        total_h = jnp.sum(row_total[h], axis=0, keepdims=True)
        qgrad_ref[rows, :] = (
            rowscale_ref[rows, :] * pulls[h]
            - rowpoint_ref[rows, :] * total_h * qt_ref[rows, :].astype(F32)
        )


def attention(kx, vals, qhi, qlo, qraw, cot, cott, qt, bias, vecs, head_dim, point_cols):
    keys = kx.shape[0]
    heads = kx.shape[1] // HEAD_COLS
    cols = qhi.shape[1]
    kw, vw = QUAD * HEAD_COLS, QUAD * head_dim
    colscale, colpoint = vecs
    by_col = lambda rows, width: pl.BlockSpec((rows, width), lambda i: (0, i))
    by_row = lambda height, width: pl.BlockSpec((height, width), lambda i: (i, 0))
    return pl.pallas_call(
        functools.partial(attention_kernel, head_dim, point_cols),
        grid=(heads // QUAD,),
        in_specs=[
            by_col(keys, kw), by_col(keys, vw), by_row(kw, cols), by_row(kw, cols),
            by_col(cols, kw), by_col(cols, vw), by_row(vw, cols), by_row(kw, cols),
            pl.BlockSpec(bias.shape, lambda i: (0, 0)),
            by_col(1, kw), by_col(1, kw), by_row(kw, 1), by_row(kw, 1),
        ],
        out_specs=[by_col(keys, kw), by_col(keys, vw), by_row(kw, cols)],
        out_shape=[
            jax.ShapeDtypeStruct((keys, heads * HEAD_COLS), BF16),
            jax.ShapeDtypeStruct((keys, heads * head_dim), BF16),
            jax.ShapeDtypeStruct((heads * HEAD_COLS, cols), F32),
        ],
        scratch_shapes=[
            pltpu.VMEM((QUAD, keys, cols), F32),
            pltpu.VMEM((QUAD, keys, cols), F32),
        ],
        compiler_params=pltpu.CompilerParams(vmem_limit_bytes=60 * 1024 * 1024),
        name="attention",
    )(kx, vals, qhi, qlo, qraw, cot, cott, qt, bias, colscale, colpoint,
      colscale.reshape(-1, 1), colpoint.reshape(-1, 1))


def split2(x):
    hi = lax.reduce_precision(x, 8, 7)
    return hi.astype(BF16), (x - hi).astype(BF16)


def head_layout(scalars, points, heads, extra):
    rows = scalars.shape[0]
    head_dim = scalars.shape[1] // heads
    count = points.shape[1] // (3 * heads)
    grid = points.reshape(rows, 3, heads, count).transpose(0, 2, 1, 3).reshape(rows, heads, 3 * count)
    pad = jnp.zeros((rows, heads, HEAD_COLS - head_dim - 3 * count - extra.shape[2]), scalars.dtype)
    parts = [scalars.reshape(rows, heads, head_dim), grid, extra, pad]
    return jnp.concatenate(parts, axis=2).reshape(rows, heads * HEAD_COLS)


def prepare(queries, query_points, keys, key_points, weights, out_grad):
    heads = weights.shape[0]
    rows, width = queries.shape
    head_dim = width // heads
    count = query_points.shape[1] // (3 * heads)
    scalar_scale = LOGIT_WEIGHT / math.sqrt(head_dim)
    point_scale = LOGIT_WEIGHT * math.sqrt(2.0 / (9.0 * count)) * weights
    wide = key_points.astype(F32).reshape(rows, 3, heads, count)
    ksq = jnp.sum(wide * wide, axis=(1, 3))
    k1 = lax.reduce_precision(ksq, 8, 7)
    k2 = lax.reduce_precision(ksq - k1, 8, 7)
    k3 = ksq - k1 - k2
    pieces = jnp.stack([k1, k2, k3], axis=2).astype(BF16)
    kx = head_layout(keys, key_points, heads, pieces)
    qraw = head_layout(queries, query_points, heads, jnp.zeros((rows, heads, 3), BF16))
    qt = qraw.T
    slot = jnp.arange(HEAD_COLS)
    is_scalar = slot < head_dim
    is_point = (slot >= head_dim) & (slot < head_dim + 3 * count)
    is_square = (slot >= head_dim + 3 * count) & (slot < head_dim + 3 * count + 3)
    a = point_scale[:, None]
    colscale = jnp.where(is_scalar, scalar_scale, jnp.where(is_point, a, 0.0)).reshape(1, -1)
    colpoint = jnp.where(is_point, a, 0.0).reshape(1, -1)
    square = jnp.where(is_square, -0.5 * a, 0.0).reshape(-1, 1)
    qhi, qlo = split2(qt.astype(F32) * colscale.reshape(-1, 1) + square)
    return kx, qraw, qt, qhi, qlo, out_grad.T, (colscale, colpoint)


def unlayout(x, heads, head_dim, count):
    rows = x.shape[0]
    x = x.reshape(rows, heads, HEAD_COLS)
    points = x[:, :, head_dim : head_dim + 3 * count].reshape(rows, heads, 3, count)
    return (
        x[:, :, :head_dim].reshape(rows, heads * head_dim),
        points.transpose(0, 2, 1, 3).reshape(rows, 3 * heads * count),
    )


def local(
    queries, query_points, keys, key_points, values, point_weights, out_grad,
    fetch_block, key_owner, key_live,
):
    owners = lax.axis_size("res")
    rows, width = queries.shape
    blocks = rows // BLOCK
    heads = point_weights.shape[0]
    head_dim = width // heads
    count = query_points.shape[1] // (3 * heads)
    kx, qraw, qt, qhi, qlo, cott, vecs = prepare(
        queries, query_points, keys, key_points, point_weights, out_grad
    )
    owner_ids = jnp.arange(owners, dtype=jnp.int32)
    named = (key_owner[:, :, None] == owner_ids) & (key_live > 0)[:, :, None]
    live = jnp.any(named, axis=1)
    bias = jnp.repeat(jnp.where(live, 0.0, -jnp.inf).astype(F32).T, BLOCK, axis=1)

    request_table = lax.all_gather(fetch_block, "res", axis=0, tiled=True)
    wanted = lax.dynamic_slice_in_dim(request_table, lax.axis_index("res"), 1, 1)[:, 0]
    packed = jnp.concatenate([kx, values], axis=1).reshape(blocks, BLOCK, -1)
    features = packed.shape[2]
    outgoing = jnp.take(packed, wanted, axis=0)
    fetched = lax.all_to_all(outgoing, "res", split_axis=0, concat_axis=0, tiled=True)
    fetched = fetched.reshape(owners * BLOCK, features)
    split = heads * HEAD_COLS
    kterm, vterm, qgrad = attention(
        fetched[:, :split], fetched[:, split:], qhi, qlo, qraw, out_grad, cott, qt, bias, vecs,
        head_dim, 3 * count,
    )
    terms = jnp.concatenate([kterm, vterm], axis=1).reshape(owners, 1, BLOCK, features)
    block_ids = jnp.arange(blocks, dtype=jnp.int32)
    chosen = (fetch_block[0][:, None] == block_ids)[:, :, None, None]
    sent = jnp.where(chosen, terms, jnp.zeros((), BF16)).reshape(owners * rows, features)
    summed = lax.psum_scatter(sent, "res", scatter_dimension=0, tiled=True).astype(F32)
    query_grad, query_point_grad = unlayout(qgrad.T, heads, head_dim, count)
    key_grad, key_point_grad = unlayout(summed[:, :split], heads, head_dim, count)
    return query_grad, query_point_grad, key_grad, key_point_grad, summed[:, split:]


def solution(mesh):
    rows = P(("grp", "res"), None)
    return jax.shard_map(
        local,
        mesh=mesh,
        in_specs=(rows,) * 5 + (P(),) + (rows,) * 4,
        out_specs=(rows,) * 5,
        check_vma=False,
    )
```

time: 629 us -> 447 us (0.71)
  matrix products: 113 us -> 0 us
  other arithmetic: 107 us -> 27.1 us
  Pallas kernels: 0 us -> 48.2 us
  local copies, waits for them, and re-layouts: 112 us -> 66.7 us
  waiting for transfers between devices: 252 us -> 261 us
    dot_general x17 -> x0, matrix products: 82.7 us -> none  [the longest x2 17.8 us: block_grads(): jnp.einsum('bhc,mhc->hbm', cot_heads, value_part, preferred_element_type=...]
    scatter-add x2 -> x0, other arithmetic: 55.1 us -> none  [per_block(): running.at[owner_row].add(slot_terms.reshape(-1, BLOCK, feature_count))]
    pallas_call x0 -> x1, Pallas kernels: none -> 48.2 us  [attention(): pl.pallas_call(functools.partial(attention_kernel, head_dim, point_cols),...]
    broadcast_in_dim x5 -> x10, local copies, waits for them, and re-layouts: 5.77 us -> 40.9 us  [the longest x5 40.2 us: local(): jnp.where(chosen, terms, jnp.zeros((), BF16))]
    sub x2 -> x0, matrix products: 30 us -> none  [block_grads(): exponent = jnp.exp(logits - highest)]
    gather x4 -> x0, local copies, waits for them, and re-layouts: 29 us -> none  [per_block(): gathered = jnp.take(fetched, owner_row, axis=0).reshape(-1, feature_count)]
    concatenate x6 -> x4, local copies, waits for them, and re-layouts: 26.3 us -> 0.89 us  [the longest x2 0.54 us: local(): packed = jnp.concatenate([kx, values], axis=1).reshape(blocks, BLOCK, -1)]
    while x30 -> x0, local copies, waits for them, and re-layouts: 19.2 us -> none
  transfers between devices with their start and end apart: 2 -> 2, of which waited for: 2 -> 2; matrix products, arithmetic and copies ran while one was open for 0% -> 2% of each run, Pallas kernels for 0% -> 0%
where the time goes in v1:
time: 447 us; the launch traced here: 446 us
  waiting for transfers between devices  261 us (58%)
  local copies, waits for them, and re-layouts  66.7 us (15%)
  Pallas kernels  48.2 us (11%)
  other arithmetic  27.1 us (6%)
  blocking collectives  23.2 us (5%)
  between operations  14.4 us (3%)
  starting transfers between devices  4.82 us (1%)
    reduce_scatter x1, waiting for transfers between devices, local(): lax.psum_scatter(sent, 'res', scatter_dimension=0, tiled=True).astype(F32)  155 us
    all_to_all x1, waiting for transfers between devices, local(): lax.all_to_all(outgoing, 'res', split_axis=0, concat_axis=0, tiled=True)  106 us
    pallas_call x1, Pallas kernels, attention(): pl.pallas_call(functools.partial(attention_kernel, head_dim, point_cols),...  48.2 us
    broadcast_in_dim x5, local copies, waits for them, and re-layouts, local(): jnp.where(chosen, terms, jnp.zeros((), BF16))  40.2 us
    all_gather x1, blocking collectives, local(): request_table = lax.all_gather(fetch_block, 'res', axis=0, tiled=True)  23.2 us
    select_n x1, other arithmetic, local(): jnp.where(chosen, terms, jnp.zeros((), BF16))  10.6 us
    unnamed x35, local copies, waits for them, and re-layouts  9.95 us
  transfers between devices with their start and end apart: 2, of which 2 were waited for; matrix products, arithmetic and copies ran while one was open for 2% of the time, Pallas kernels for 0%

profile of v1, /device:TPU:0, one launch (start us, length us, event | category | flops | bytes accessed | tf_op | source)
XLA Modules:
  0.0 445.7 jit_solution(18313631229640963600)
XLA Ops:
  7.2 23.2 %all-gather = s32[16,1,16]{2,1,0:T(1,128)S(1)} all-gather(s32[1,1,16]{2,1,0:T(1,128)} %bitcast.91), channel_id=1, replica_groups=mesh['grp'=2,'res'=16] {'res'}, dimensions={0}, use_global_device_ids=true | all-gather | bytes 1088 | tf_op jit(solution)/shard_map/all_gather | solution.py:253
  30.8 1.1 copy.117
  31.9 1.1 copy.118
  34.0 1.0 pad_maximum_fusion.1
  35.0 3.6 gather_fusion
  38.6 6.1 %broadcast_select_fusion.1 = bf16[16,128,1536]{2,1,0:T(8,128)(2,1)} fusion(bf16[16,128,1536]{2,1,0:T(8,128)(2,1)} %gather_fusion, pred[16]{0:T(512)(128)(4,1)S(1)} %and_bitcast_fusion), kind=kLoop, calls=%fused_computation.3 | loop fusion | flops 3145728 | bytes 12582928 | tf_op jit(solution)/shard_map/jit(_take)/select_n | solution.py:257
  44.8 4.8 %all-to-all-start = ((bf16[16,128,1536]{2,1,0:T(8,128)(2,1)}), bf16[16,128,1536]{2,1,0:T(8,128)(2,1)}, u32[]{:S(2)}, u32[]{:S(2)}) async-start(bf16[16,128,1536]{2,1,0:T(8,128)(2,1)} %broadcast_select_fusion.1), calls=%async_computation | async-start | bytes 12582912 | tf_op jit(solution)/shard_map/all_to_all | solution.py:258
  49.7 0.5 broadcast_in_dim.132
  50.5 0.5 select_n.113.rowpoint_ref
  51.8 1.0 copy.132.qraw_ref
  52.8 0.8 copy.128
  53.9 0.6 copy.148
  54.7 0.6 broadcast_select_fusion.6.colscale_ref
  55.3 0.9 broadcast_select_fusion.2.rowscale_ref
  56.2 1.3 fusion
  57.5 106.2 %all-to-all-done = bf16[16,128,1536]{2,1,0:T(8,128)(2,1)} async-done(((bf16[16,128,1536]{2,1,0:T(8,128)(2,1)}), bf16[16,128,1536]{2,1,0:T(8,128)(2,1)}, u32[]{:S(2)}, u32[]{:S(2)}) %all-to-all-start) | async-done | bytes 6291488 | tf_op jit(solution)/shard_map/all_to_all | solution.py:258
  163.7 4.6 %slice.34.kx_ref = bf16[2048,1024]{1,0:T(8,128)(2,1)} slice(bf16[2048,1536]{1,0:T(8,128)(2,1)} %bitcast.10), slice={[0:2048], [0:1024]} | slice | bytes 8388608 | tf_op jit(solution)/shard_map/slice | solution.py:262
  168.3 3.0 slice.35.v_ref
  171.4 48.2 %attention.1 = (bf16[2048,1024]{1,0:T(8,128)(2,1)}, bf16[2048,512]{1,0:T(8,128)(2,1)}, f32[1024,256]{1,0:T(8,128)}) custom-call(bf16[2048,1024]{1,0:T(8,128)(2,1)} %slice.34.kx_ref, bf16[2048,512]{1,0:T(8,128)(2,1)} %slice.35.v_ref, bf16[1024,256]{1,0:T(8,128)(2,1)} %get-tuple-element.37.qhi_ref, bf16[1024,256]{1,0:T(8,128)(2,1)} %get-tuple-element.36.qlo_ref, ...), custom_call_target="tpu_custom_call" | custom-call | tf_op jit(solution)/shard_map/attention/pallas_call | solution.py:157
  219.6 6.0 %pad_maximum_fusion = bf16[2048,1536]{1,0:T(8,128)(2,1)} fusion(bf16[2048,512]{1,0:T(8,128)(2,1)} %get-tuple-element.10, bf16[2048,1024]{1,0:T(8,128)(2,1)} %get-tuple-element.9), kind=kLoop, calls=%fused_computation.2 | loop fusion | flops 12582912 | bytes 12582912 | tf_op jit(solution)/shard_map/concatenate | solution.py:265
  225.6 9.1 %copy.135 = bf16[16,128,1536]{1,0,2:T(8,128)(2,1)} copy(bf16[16,128,1536]{2,1,0:T(8,128)(2,1)} %bitcast.69) | data formatting | bytes 12582912 | tf_op jit(solution)/shard_map/jit(_where)/broadcast_in_dim | solution.py:268
  234.7 9.9 %broadcast_in_dim.129 = bf16[16,2,128,1536]{2,1,0,3:T(2,128)(2,1)} broadcast(bf16[16,128,1536]{1,0,2:T(8,128)(2,1)} %copy.135), dimensions={0,2,3} | broadcast | bytes 18874368 | tf_op jit(solution)/shard_map/jit(_where)/broadcast_in_dim | solution.py:268
  244.6 21.1 %broadcast_in_dim.130 = bf16[4096,1536]{0,1:T(8,128)(2,1)} reshape(bf16[16,2,128,1536]{2,1,0,3:T(2,128)(2,1)} %broadcast_in_dim.129) | data formatting | bytes 25165824 | tf_op jit(solution)/shard_map/jit(_where)/broadcast_in_dim | solution.py:268
  265.7 10.6 %broadcast_select_fusion = bf16[4096,1536]{0,1:T(8,128)(2,1)} fusion(bf16[4096,1536]{0,1:T(8,128)(2,1)} %broadcast_in_dim.130, pred[4096]{0:T(1024)(128)(4,1)S(1)} %broadcast_in_dim.126), kind=kLoop, calls=%fused_computation.1 | loop fusion | flops 6291456 | bytes 25169920 | tf_op jit(solution)/shard_map/jit(_where)/select_n | solution.py:268
  276.3 1.2 copy-done.4
  277.6 1.0 copy.137
  278.6 0.9 copy.138
  279.5 155.0 %reduce-scatter.2.cloned.1.call-done = bf16[256,1536]{0,1:T(8,128)(2,1)} async-done(((bf16[4096,1536]{0,1:T(8,128)(2,1)}), bf16[256,1536]{0,1:T(8,128)(2,1)}) %reduce-scatter.2.cloned.1.call-update) | async-done | bytes 786448 | tf_op jit(solution)/shard_map/reduce_scatter | solution.py:269
  434.6 1.2 slice.38
  435.8 1.0 copy.139
  436.9 0.9 copy.140
  437.8 1.0 copy.141
  (71 shorter events, 3.2 us)
Async XLA Ops:
  44.7 5.6 %copy-start.11 = (f32[16]{0:T(128)S(1)}, f32[16]{0:T(128)}, u32[]{:S(2)}) copy-start(f32[16]{0:T(128)} %param.15) | copy-start | bytes 196
  44.7 6.4 %copy-start.6 = (bf16[256,384]{1,0:T(8,128)(2,1)S(1)}, bf16[256,384]{1,0:T(8,128)(2,1)}, u32[]{:S(2)}) copy-start(bf16[256,384]{1,0:T(8,128)(2,1)} %param.11) | copy-start | bytes 589828
  44.7 6.5 %copy-start.5 = (bf16[256,512]{1,0:T(8,128)(2,1)S(1)}, bf16[256,512]{1,0:T(8,128)(2,1)}, u32[]{:S(2)}) copy-start(bf16[256,512]{1,0:T(8,128)(2,1)} %param.10) | copy-start | bytes 786436
  44.7 8.0 %copy-start.3 = (bf16[256,512]{1,0:T(8,128)(2,1)S(1)}, bf16[256,512]{1,0:T(8,128)(2,1)}, u32[]{:S(2)}) copy-start(bf16[256,512]{1,0:T(8,128)(2,1)} %cot_ref.1) | copy-start | bytes 786436
  44.8 8.9 %copy-start.10 = (s32[2,16]{1,0:T(2,128)S(1)}, s32[2,16]{1,0:T(2,128)}, u32[]{:S(2)}) copy-start(s32[2,16]{1,0:T(2,128)} %param.19) | copy-start | bytes 388
  44.8 8.8 %copy-start.9 = (s32[2,16]{1,0:T(2,128)S(1)}, s32[2,16]{1,0:T(2,128)}, u32[]{:S(2)}) copy-start(s32[2,16]{1,0:T(2,128)} %param.18) | copy-start | bytes 388
  44.8 9.7 %copy-start.8 = (s32[1,16]{1,0:T(1,128)S(1)}, s32[1,16]{1,0:T(1,128)}, u32[]{:S(2)}) copy-start(s32[1,16]{1,0:T(1,128)} %param.17) | copy-start | bytes 196
  44.8 118.9 %all-to-all-start = ((bf16[16,128,1536]{2,1,0:T(8,128)(2,1)}), bf16[16,128,1536]{2,1,0:T(8,128)(2,1)}, u32[]{:S(2)}, u32[]{:S(2)}) async-start(bf16[16,128,1536]{2,1,0:T(8,128)(2,1)} %broadcast_select_fusion.1), calls=%async_computation | async-start | bytes 12582912 | tf_op jit(solution)/shard_map/all_to_all | solution.py:258
  49.6 385.0 %reduce-scatter.2.cloned.1.call-start = ((), (), s32[]{:S(2)}) async-start(), calls=%async_computation.2 | async-start | bytes 13369344 | tf_op jit(solution)/shard_map/reduce_scatter | solution.py:269
  50.5 117.9 %copy-start.7 = (f32[1,1024]{1,0:T(1,128)}, f32[1,1024]{1,0:T(1,128)S(1)}, u32[]{:S(2)}) copy-start(f32[1,1024]{1,0:T(1,128)S(1)} %select_n.108.colpoint_ref) | copy-start | bytes 12292
  51.0 117.4 %copy-start.1 = (f32[1024,1]{1,0:T(8,128)}, f32[1024,1]{1,0:T(8,128)S(1)}, u32[]{:S(2)}) copy-start(f32[1024,1]{1,0:T(8,128)S(1)} %select_n.113.rowpoint_ref) | copy-start | bytes 12292
  51.7 116.6 %copy-start = (bf16[256,16,64]{0,2,1:T(8,128)(2,1)}, bf16[256,16,64]{0,2,1:T(8,128)(2,1)S(1)}, u32[]{:S(2)}) copy-start(bf16[256,16,64]{0,2,1:T(8,128)(2,1)S(1)} %pad_maximum_fusion.2) | copy-start | bytes 1572868
  276.3 1.2 copy-start.4
  434.6 3.2 copy-start.2
Sparse Core Ops, SparseCore 0:
  276.4 158.0 reduce-scatter.1

commit v2 on v1

--- a/solution.py
+++ b/solution.py
@@ -26,11 +26,12 @@
 
 
 def attention_kernel(
-    head_dim, point_cols, kx_ref, v_ref, qhi_ref, qlo_ref, qraw_ref, cot_ref, cott_ref, qt_ref,
+    head_dim, pick_ref, g_ref, qhi_ref, qlo_ref, qraw_ref, cot_ref, cott_ref, qt_ref,
     bias_ref, colscale_ref, colpoint_ref, rowscale_ref, rowpoint_ref,
-    kterm_ref, vterm_ref, qgrad_ref, s_ref, d_ref,
+    term_ref, qgrad_ref, s_ref, d_ref,
 ):
-    keys = kx_ref.shape[0]
+    keys = s_ref.shape[1]
+    wide = QUAD * HEAD_COLS
     cols = qhi_ref.shape[1]
     chunks = keys // CHUNK
     zeros = jnp.zeros((HEAD_COLS, cols), BF16)
@@ -46,6 +47,18 @@
         keep = (row >= h * head_dim) & (row < (h + 1) * head_dim)
         return jnp.where(keep, cott_ref[...], jnp.zeros((), BF16))
 
+    def load(i, span):
+        first = g_ref[0, 2 * i, pick_ref[2 * i], :, span]
+        second = g_ref[0, 2 * i + 1, pick_ref[2 * i + 1], :, span]
+        return jnp.concatenate([first, second], axis=0)
+
+    def store(i, span, value):
+        for j in range(2):
+            o = 2 * i + j
+            part = value[j * BLOCK : (j + 1) * BLOCK].astype(BF16)
+            term_ref[0, o, pick_ref[o], :, span] = part
+            term_ref[0, o, 1 - pick_ref[o], :, span] = jnp.zeros_like(part)
+
     qw = [score_weights(h) for h in range(QUAD)]
     ow = [cot_weights(h) for h in range(QUAD)]
 
@@ -53,10 +66,10 @@
         rows = pl.ds(pl.multiple_of(i * CHUNK, CHUNK), CHUNK)
         low = bias_ref[pl.ds(i * 2, 1), :]
         high = bias_ref[pl.ds(i * 2 + 1, 1), :]
-        vals = v_ref[rows, :]
+        vals = load(i, slice(wide, wide + 128))
         out = []
         for h in range(QUAD):
-            pair = kx_ref[rows, (h // 2) * 128 : (h // 2 + 1) * 128]
+            pair = load(i, slice((h // 2) * 128, (h // 2 + 1) * 128))
             s = dot(jnp.concatenate([pair, pair], axis=1), qw[h])
             s = jnp.concatenate([s[:BLOCK] + low, s[BLOCK:] + high], axis=0)
             s_ref[h, rows, :] = s
@@ -109,7 +122,7 @@
         new_total, new_pulls = [], []
         vterm = None
         for g in range(QUAD // 2):
-            pair = kx_ref[rows, g * 128 : (g + 1) * 128]
+            pair = load(i, slice(g * 128, (g + 1) * 128))
             kterm = None
             col_totals = []
             for h in (2 * g, 2 * g + 1):
@@ -131,8 +144,8 @@
             sums = jnp.where(half, col_totals[0], col_totals[1])
             span = slice(g * 128, (g + 1) * 128)
             kterm = colscale_ref[:, span] * kterm - colpoint_ref[:, span] * sums * pair.astype(F32)
-            kterm_ref[rows, span] = kterm.astype(BF16)
-        vterm_ref[rows, :] = vterm.astype(BF16)
+            store(i, span, kterm)
+        store(i, slice(wide, wide + 128), vterm)
         return tuple(new_total), tuple(new_pulls)
 
     pull0 = tuple(jnp.zeros((HEAD_COLS, cols), F32) for _ in range(QUAD))
@@ -146,37 +159,331 @@
         )
 
 
-def attention(kx, vals, qhi, qlo, qraw, cot, cott, qt, bias, vecs, head_dim, point_cols):
-    keys = kx.shape[0]
-    heads = kx.shape[1] // HEAD_COLS
+def attention(gathered, pick, qhi, qlo, qraw, cot, cott, qt, bias, vecs, head_dim):
+    quads, owners, rows, features = gathered.shape
+    keys = owners * BLOCK
     cols = qhi.shape[1]
     kw, vw = QUAD * HEAD_COLS, QUAD * head_dim
     colscale, colpoint = vecs
-    by_col = lambda rows, width: pl.BlockSpec((rows, width), lambda i: (0, i))
-    by_row = lambda height, width: pl.BlockSpec((height, width), lambda i: (i, 0))
-    return pl.pallas_call(
-        functools.partial(attention_kernel, head_dim, point_cols),
-        grid=(heads // QUAD,),
-        in_specs=[
-            by_col(keys, kw), by_col(keys, vw), by_row(kw, cols), by_row(kw, cols),
-            by_col(cols, kw), by_col(cols, vw), by_row(vw, cols), by_row(kw, cols),
-            pl.BlockSpec(bias.shape, lambda i: (0, 0)),
-            by_col(1, kw), by_col(1, kw), by_row(kw, 1), by_row(kw, 1),
-        ],
-        out_specs=[by_col(keys, kw), by_col(keys, vw), by_row(kw, cols)],
+    by_col = lambda height, width: pl.BlockSpec((height, width), lambda i, _: (0, i))
+    by_row = lambda height, width: pl.BlockSpec((height, width), lambda i, _: (i, 0))
+    blocks = pl.BlockSpec(
+        (1, owners, rows // BLOCK, BLOCK, features),
+        lambda i, _: (i, 0, 0, 0, 0),
+        pipeline_mode=pl.Buffered(1 if owners > 16 else 2),
+    )
+    shape = (quads, owners, rows // BLOCK, BLOCK, features)
+    terms, qgrad = pl.pallas_call(
+        functools.partial(attention_kernel, head_dim),
+        grid_spec=pltpu.PrefetchScalarGridSpec(
+            num_scalar_prefetch=1,
+            grid=(quads,),
+            in_specs=[
+                blocks, by_row(kw, cols), by_row(kw, cols),
+                by_col(cols, kw), by_col(cols, vw), by_row(vw, cols), by_row(kw, cols),
+                pl.BlockSpec(bias.shape, lambda i, _: (0, 0)),
+                by_col(1, kw), by_col(1, kw), by_row(kw, 1), by_row(kw, 1),
+            ],
+            out_specs=[blocks, by_row(kw, cols)],
+            scratch_shapes=[
+                pltpu.VMEM((QUAD, keys, cols), F32),
+                pltpu.VMEM((QUAD, keys, cols), F32),
+            ],
+        ),
         out_shape=[
-            jax.ShapeDtypeStruct((keys, heads * HEAD_COLS), BF16),
-            jax.ShapeDtypeStruct((keys, heads * head_dim), BF16),
-            jax.ShapeDtypeStruct((heads * HEAD_COLS, cols), F32),
-        ],
-        scratch_shapes=[
-            pltpu.VMEM((QUAD, keys, cols), F32),
-            pltpu.VMEM((QUAD, keys, cols), F32),
+            jax.ShapeDtypeStruct(shape, BF16),
+            jax.ShapeDtypeStruct((quads * kw, cols), F32),
         ],
         compiler_params=pltpu.CompilerParams(vmem_limit_bytes=60 * 1024 * 1024),
         name="attention",
-    )(kx, vals, qhi, qlo, qraw, cot, cott, qt, bias, colscale, colpoint,
+    )(pick, gathered.reshape(shape), qhi, qlo, qraw, cot, cott, qt, bias, colscale, colpoint,
       colscale.reshape(-1, 1), colpoint.reshape(-1, 1))
+    return terms.reshape(gathered.shape), qgrad
+
+
+def place():
+    me = lax.axis_index("res")
+    return me, me // 4, (me // 2) % 2, me % 2
+
+
+def greet(a, depth, side, sibling, me):
+    barrier = pltpu.get_barrier_semaphore()
+
+    def signal(target):
+        pl.semaphore_signal(
+            barrier, inc=1, device_id={"res": target}, device_id_type=pl.DeviceIdType.MESH
+        )
+
+    signal(side)
+    signal(sibling)
+    pl.when(a > 0)(lambda: signal(me - 4))
+    pl.when(a < depth - 1)(lambda: signal(me + 4))
+    peers = 2 + jnp.where(a > 0, 1, 0) + jnp.where(a < depth - 1, 1, 0)
+    pl.semaphore_wait(barrier, peers)
+
+
+def remote(src, dst, send_sem, recv_sem, target):
+    return pltpu.make_async_remote_copy(
+        src_ref=src, dst_ref=dst, send_sem=send_sem, recv_sem=recv_sem,
+        device_id={"res": target}, device_id_type=pl.DeviceIdType.MESH,
+    )
+
+
+UP, DOWN, SIDE, SIBLING = range(4)
+
+
+def gather_kernel(depth, x_ref, g_ref, send_sem, recv_sem, local_sem):
+    quads = x_ref.shape[0]
+    me, a, b, c = place()
+    side = me + 2 - 4 * b
+    sibling = me + 1 - 2 * c
+    targets = {UP: me + 4, DOWN: me - 4, SIDE: side, SIBLING: sibling}
+    can = {UP: a < depth - 1, DOWN: a > 0}
+    greet(a, depth, side, sibling, me)
+
+    def send(way, slot, q, own=False):
+        src = x_ref.at[q] if own else g_ref.at[q, slot]
+        return remote(
+            src, g_ref.at[q, slot], send_sem.at[way, slot, q], recv_sem.at[slot, q], targets[way]
+        )
+
+    def each(fn):
+        def body(q, carry):
+            fn(q)
+            return carry
+        lax.fori_loop(0, quads, body, 0)
+
+    def pass_on(ways, slot, q, own=False):
+        for way in ways:
+            if way in can:
+                pl.when(can[way])(lambda way=way: send(way, slot, q, own).start())
+            else:
+                send(way, slot, q, own).start()
+
+    def settle(ways, slot, q, own=False):
+        for way in ways:
+            if way in can:
+                pl.when(can[way])(lambda way=way: send(way, slot, q, own).wait_send())
+            else:
+                send(way, slot, q, own).wait_send()
+
+    def arrive(slot, q):
+        send(SIBLING, slot, q).wait_recv()
+
+    def own_copy(q):
+        return pltpu.make_async_copy(x_ref.at[q], g_ref.at[q, me], local_sem.at[q])
+
+    def start(q):
+        pass_on((UP, DOWN, SIDE, SIBLING), me, q, True)
+        own_copy(q).start()
+
+    each(start)
+    routes = []
+    for step in range(1, depth + 1):
+        if step < depth:
+            routes.append((a - step >= 0, me - 4 * step, (UP, SIDE, SIBLING)))
+            routes.append((a + step < depth, me + 4 * step, (DOWN, SIDE, SIBLING)))
+        near = step - 1
+        routes.append((a - near >= 0, side - 4 * near, (SIBLING,)))
+        if near:
+            routes.append((a + near < depth, side + 4 * near, (SIBLING,)))
+
+    for valid, slot, ways in routes:
+        @pl.when(valid)
+        def _(slot=slot, ways=ways):
+            def go(q):
+                arrive(slot, q)
+                pass_on(ways, slot, q)
+            each(go)
+
+    def finish(q):
+        def body(i, carry):
+            arrive(2 * i + 1 - c, q)
+            return carry
+        lax.fori_loop(0, 2 * depth, body, 0)
+        settle((UP, DOWN, SIDE, SIBLING), me, q, True)
+        own_copy(q).wait()
+
+    each(finish)
+    for valid, slot, ways in routes:
+        @pl.when(valid)
+        def _(slot=slot, ways=ways):
+            each(lambda q: settle(ways, slot, q))
+
+
+def gather(x, owners):
+    quads, rows, features = x.shape
+    hbm = pl.BlockSpec(memory_space=pl.ANY)
+    return pl.pallas_call(
+        functools.partial(gather_kernel, owners // 4),
+        in_specs=[hbm],
+        out_specs=hbm,
+        out_shape=jax.ShapeDtypeStruct((quads, owners, rows, features), x.dtype),
+        scratch_shapes=[
+            pltpu.SemaphoreType.DMA((4, owners, quads)),
+            pltpu.SemaphoreType.DMA((owners, quads)),
+            pltpu.SemaphoreType.DMA((quads,)),
+        ],
+        compiler_params=pltpu.CompilerParams(collective_id=0, has_side_effects=True),
+        name="gather_blocks",
+    )(x)
+
+
+def scatter_kernel(
+    depth, t_ref, out_ref, acc, from_core, from_side, from_low, from_high,
+    local_sem, core_send, core_recv, side_send, side_recv, up_send, low_recv, down_send, high_recv,
+):
+    quads = t_ref.shape[0]
+    me, a, b, c = place()
+    side = me + 2 - 4 * b
+    sibling = me + 1 - 2 * c
+    greet(a, depth, side, sibling, me)
+
+    def own_copy(q, dest):
+        return pltpu.make_async_copy(
+            t_ref.at[q, 2 * dest + c], acc.at[q, dest], local_sem.at[q, dest]
+        )
+
+    def core_copy(q, dest):
+        return remote(
+            t_ref.at[q, 2 * dest + 1 - c], from_core.at[q, dest],
+            core_send.at[q, dest], core_recv.at[q, dest], sibling,
+        )
+
+    def side_copy(q, z):
+        return remote(
+            acc.at[q, 2 * z + 1 - b], from_side.at[q, z], side_send.at[q, z], side_recv.at[q, z], side
+        )
+
+    def up_copy(q, z):
+        return remote(
+            acc.at[q, 2 * z + b], from_low.at[q, z], up_send.at[q, z], low_recv.at[q, z], me + 4
+        )
+
+    def down_copy(q, z):
+        return remote(
+            acc.at[q, 2 * z + b], from_high.at[q, z], down_send.at[q, z], high_recv.at[q, z], me - 4
+        )
+
+    def each(fn):
+        def body(q, carry):
+            fn(q)
+            return carry
+        lax.fori_loop(0, quads, body, 0)
+
+    def every(fn):
+        for step in range(depth - 1, 0, -1):
+            pl.when(a + step < depth)(lambda: fn(a + step, 1))
+            pl.when(a - step >= 0)(lambda: fn(a - step, -1))
+        fn(a, 0)
+
+    def begin(z, _):
+        def go(q):
+            for lane in (1 - b, b):
+                core_copy(q, 2 * z + lane).start()
+                own_copy(q, 2 * z + lane).start()
+        each(go)
+
+    every(begin)
+
+    def arrived(q, dest):
+        own_copy(q, dest).wait()
+        core_copy(q, dest).wait_recv()
+
+    def across(z, _):
+        def go(q):
+            dest = 2 * z + 1 - b
+            arrived(q, dest)
+            acc[q, dest] = (acc[q, dest].astype(F32) + from_core[q, dest].astype(F32)).astype(BF16)
+            side_copy(q, z).start()
+        each(go)
+
+    every(across)
+
+    def along(z, way):
+        def go(q):
+            dest = 2 * z + b
+            arrived(q, dest)
+            side_copy(q, z).wait_recv()
+
+            def total():
+                part = acc[q, dest].astype(F32) + from_core[q, dest].astype(F32)
+                return part + from_side[q, z].astype(F32)
+
+            def put(value):
+                if way == 0:
+                    out_ref[q] = value
+                else:
+                    acc[q, dest] = value.astype(BF16)
+
+            def below():
+                up_copy(q, z).wait_recv()
+                return from_low[q, z].astype(F32)
+
+            def above():
+                down_copy(q, z).wait_recv()
+                return from_high[q, z].astype(F32)
+
+            if way == 1:
+                pl.when(a > 0)(lambda: put(total() + below()))
+                pl.when(a == 0)(lambda: put(total()))
+                up_copy(q, z).start()
+            elif way == -1:
+                pl.when(a < depth - 1)(lambda: put(total() + above()))
+                pl.when(a == depth - 1)(lambda: put(total()))
+                down_copy(q, z).start()
+            else:
+                put(total())
+
+                @pl.when(a > 0)
+                def _():
+                    out_ref[q] += below()
+
+                @pl.when(a < depth - 1)
+                def _():
+                    out_ref[q] += above()
+        each(go)
+
+    every(along)
+
+    def settle(z, way):
+        def go(q):
+            for lane in (1 - b, b):
+                core_copy(q, 2 * z + lane).wait_send()
+            side_copy(q, z).wait_send()
+            if way == 1:
+                up_copy(q, z).wait_send()
+            elif way == -1:
+                down_copy(q, z).wait_send()
+        each(go)
+
+    every(settle)
+
+
+def scatter_sum(terms):
+    quads, owners, rows, features = terms.shape
+    depth = owners // 4
+    tile = (rows, features)
+    dma = pltpu.SemaphoreType.DMA
+    return pl.pallas_call(
+        functools.partial(scatter_kernel, depth),
+        in_specs=[pl.BlockSpec(memory_space=pl.ANY)],
+        out_specs=pl.BlockSpec(memory_space=pltpu.VMEM),
+        out_shape=jax.ShapeDtypeStruct((quads, rows, features), F32),
+        scratch_shapes=[
+            pltpu.VMEM((quads, 2 * depth) + tile, BF16),
+            pltpu.VMEM((quads, 2 * depth) + tile, BF16),
+            pltpu.VMEM((quads, depth) + tile, BF16),
+            pltpu.VMEM((quads, depth) + tile, BF16),
+            pltpu.VMEM((quads, depth) + tile, BF16),
+        ]
+        + [dma((quads, 2 * depth))] * 3
+        + [dma((quads, depth))] * 6,
+        compiler_params=pltpu.CompilerParams(
+            collective_id=1, has_side_effects=True, vmem_limit_bytes=60 * 1024 * 1024
+        ),
+        name="scatter_sums",
+    )(terms)
 
 
 def split2(x):
@@ -250,26 +557,18 @@
     live = jnp.any(named, axis=1)
     bias = jnp.repeat(jnp.where(live, 0.0, -jnp.inf).astype(F32).T, BLOCK, axis=1)
 
-    request_table = lax.all_gather(fetch_block, "res", axis=0, tiled=True)
-    wanted = lax.dynamic_slice_in_dim(request_table, lax.axis_index("res"), 1, 1)[:, 0]
-    packed = jnp.concatenate([kx, values], axis=1).reshape(blocks, BLOCK, -1)
-    features = packed.shape[2]
-    outgoing = jnp.take(packed, wanted, axis=0)
-    fetched = lax.all_to_all(outgoing, "res", split_axis=0, concat_axis=0, tiled=True)
-    fetched = fetched.reshape(owners * BLOCK, features)
-    split = heads * HEAD_COLS
-    kterm, vterm, qgrad = attention(
-        fetched[:, :split], fetched[:, split:], qhi, qlo, qraw, out_grad, cott, qt, bias, vecs,
-        head_dim, 3 * count,
-    )
-    terms = jnp.concatenate([kterm, vterm], axis=1).reshape(owners, 1, BLOCK, features)
-    block_ids = jnp.arange(blocks, dtype=jnp.int32)
-    chosen = (fetch_block[0][:, None] == block_ids)[:, :, None, None]
-    sent = jnp.where(chosen, terms, jnp.zeros((), BF16)).reshape(owners * rows, features)
-    summed = lax.psum_scatter(sent, "res", scatter_dimension=0, tiled=True).astype(F32)
+    quads = heads // QUAD
+    by_quad = [kx.reshape(rows, quads, -1), values.reshape(rows, quads, -1)]
+    packed = jnp.concatenate(by_quad, axis=2).transpose(1, 0, 2)
+    gathered = gather(packed, owners)
+    terms, qgrad = attention(
+        gathered, fetch_block[0], qhi, qlo, qraw, out_grad, cott, qt, bias, vecs, head_dim
+    )
+    summed = scatter_sum(terms).transpose(1, 0, 2)
     query_grad, query_point_grad = unlayout(qgrad.T, heads, head_dim, count)
-    key_grad, key_point_grad = unlayout(summed[:, :split], heads, head_dim, count)
-    return query_grad, query_point_grad, key_grad, key_point_grad, summed[:, split:]
+    split = QUAD * HEAD_COLS
+    key_grad, key_point_grad = unlayout(summed[:, :, :split], heads, head_dim, count)
+    return query_grad, query_point_grad, key_grad, key_point_grad, summed[:, :, split:].reshape(rows, width)
 
 
 def solution(mesh):

time: 447 us -> 223 us (0.50)
  waiting for transfers between devices: 261 us -> 0 us
  Pallas kernels: 48.2 us -> 202 us
  local copies, waits for them, and re-layouts: 66.7 us -> 13.1 us
  blocking collectives: 23.2 us -> 0 us
  other arithmetic: 27.1 us -> 6.43 us
  between operations: 14.4 us -> 0.99 us
  starting transfers between devices: 4.82 us -> 0 us
    reduce_scatter x1 -> x0, waiting for transfers between devices: 155 us -> none  [local(): lax.psum_scatter(sent, 'res', scatter_dimension=0, tiled=True).astype(F32)]
    pallas_call x1 -> x3, Pallas kernels: 48.2 us -> 202 us  [the longest x1 77 us: gather(): pl.pallas_call(functools.partial(gather_kernel, owners // 4), in_specs=[h...]
    all_to_all x1 -> x0, waiting for transfers between devices: 106 us -> none  [local(): lax.all_to_all(outgoing, 'res', split_axis=0, concat_axis=0, tiled=True)]
    broadcast_in_dim x5 -> x0, local copies, waits for them, and re-layouts: 40.2 us -> none  [local(): jnp.where(chosen, terms, jnp.zeros((), BF16))]
    all_gather x1 -> x0, blocking collectives: 23.2 us -> none  [local(): request_table = lax.all_gather(fetch_block, 'res', axis=0, tiled=True)]
    select_n x3 -> x0, other arithmetic: 16.7 us -> none  [the longest x1 10.6 us: local(): jnp.where(chosen, terms, jnp.zeros((), BF16))]
    slice x4, local copies, waits for them, and re-layouts: 8.9 us -> 0.64 us  [the longest x2 0.41 us: local(): summed[:, :, :split]]
    concatenate x2 -> x0, other arithmetic: 7.05 us -> none  [the longest x1 6.05 us: local(): jnp.concatenate([kterm, vterm], axis=1).reshape(owners, 1, BLOCK, features)]
  transfers between devices with their start and end apart: 2 -> 0, of which waited for: 2 -> 0; matrix products, arithmetic and copies ran while one was open for 2% -> 0% of each run, Pallas kernels for 0% -> 0%
where the time goes in v2:
time: 223 us
  Pallas kernels  202 us (91%)
  local copies, waits for them, and re-layouts  13.1 us (6%)
  other arithmetic  6.43 us (3%)
    pallas_call x1, Pallas kernels, gather(): pl.pallas_call(functools.partial(gather_kernel, owners // 4), in_specs=[h...  77 us
    pallas_call x1, Pallas kernels, scatter_sum(): pl.pallas_call(functools.partial(scatter_kernel, depth), in_specs=[pl.Blo...  75.4 us
    pallas_call x1, Pallas kernels, attention(): pl.pallas_call(functools.partial(attention_kernel, head_dim), grid_spec=p...  49.6 us
    unnamed x30, local copies, waits for them, and re-layouts  9 us

profile of v2, /device:TPU:0, one launch (start us, length us, event | category | flops | bytes accessed | tf_op | source)
XLA Modules:
  0.0 222.6 jit_solution(12248604307193791850)
XLA Ops:
  0.7 0.7 broadcast_compare_fusion
  1.4 0.8 fusion.3
  2.3 0.7 broadcast_multiply_fusion.1
  2.9 0.1 broadcast_in_dim.79
  3.2 0.6 copy.109
  4.0 0.6 broadcast_select_fusion.4.colscale_ref
  4.7 0.5 broadcast_in_dim.83
  5.2 1.1 copy.76
  6.4 1.1 copy.86
  7.5 0.1 copy.85
  7.7 0.2 pad_maximum_fusion
  7.9 0.1 copy.75
  8.1 0.1 copy.82
  8.2 0.2 copy.84
  8.5 0.8 copy.88
  9.5 0.3 concatenate.10
  9.8 0.2 copy.83
  10.0 1.0 maximum_bitcast_fusion.x_ref
  11.0 0.5 select_n.90.rowpoint_ref
  11.5 1.0 broadcast_select_fusion.rowscale_ref
  12.4 1.0 copy.92.qraw_ref
  13.4 1.3 fusion
  14.8 77.0 %gather_blocks.1 = bf16[4,16,256,384]{3,2,1,0:T(8,128)(2,1)} custom-call(bf16[4,256,384]{2,1,0:T(8,128)(2,1)} %maximum_bitcast_fusion.x_ref), custom_call_target="tpu_custom_call" | custom-call | tf_op jit(solution)/shard_map/gather_blocks/pallas_call | solution.py:317
  91.8 49.6 %attention.1 = (bf16[4,16,2,128,384]{4,3,2,1,0:T(8,128)(2,1)}, f32[1024,256]{1,0:T(8,128)}) custom-call(s32[16]{0:T(128)} %bitcast.86, bf16[4,16,2,128,384]{4,3,2,1,0:T(8,128)(2,1)} %bitcast.59, bf16[1024,256]{1,0:T(8,128)(2,1)} %get-tuple-element.25.qhi_ref, bf16[1024,256]{1,0:T(8,128)(2,1)} %get-tuple-element.24.qlo_ref, bf16[256,1024]{1,0:T(8,128)(2,1)} %copy.92.qraw_ref, ...), custom_call_target="tpu_custom_call" | custom-call | tf_op jit(solution)/shard_map/attention/pallas_call | solution.py:176
  141.4 75.4 %scatter_sums.1 = f32[4,256,384]{2,1,0:T(8,128)} custom-call(bf16[4,16,256,384]{3,2,1,0:T(8,128)(2,1)} %bitcast.60), custom_call_target="tpu_custom_call" | custom-call | tf_op jit(solution)/shard_map/scatter_sums/pallas_call | solution.py:468
  216.9 1.0 copy.98
  218.0 0.9 copy.99
  219.0 0.3 copy.95
  219.4 0.2 copy.97
  219.6 1.0 copy.102
  220.6 1.0 copy.100
  221.7 0.9 copy.101
  (48 shorter events, 1.1 us)
Async XLA Ops:
  0.6 6.9 %copy-start.5 = (bf16[256,512]{1,0:T(8,128)(2,1)S(1)}, bf16[256,512]{1,0:T(8,128)(2,1)}, u32[]{:S(2)}) copy-start(bf16[256,512]{1,0:T(8,128)(2,1)} %param.10) | copy-start | bytes 786436
  4.0 3.9 %copy-start.8 = (f32[1,1024]{1,0:T(1,128)}, f32[1,1024]{1,0:T(1,128)S(1)}, u32[]{:S(2)}) copy-start(f32[1,1024]{1,0:T(1,128)S(1)} %select_n.86.colpoint_ref) | copy-start | bytes 12292
  5.2 2.7 %copy-start.6 = (bf16[256,512]{1,0:T(8,128)(2,1)S(1)}, bf16[256,512]{1,0:T(8,128)(2,1)}, u32[]{:S(2)}) copy-start(bf16[256,512]{1,0:T(8,128)(2,1)} %param.12) | copy-start | bytes 786436
  6.4 1.7 copy-start.7
  7.5 1.0 copy-start.3
  7.9 5.5 %copy-start = (bf16[256,16,64]{0,2,1:T(8,128)(2,1)}, bf16[256,16,64]{0,2,1:T(8,128)(2,1)S(1)}, u32[]{:S(2)}) copy-start(bf16[256,16,64]{0,2,1:T(8,128)(2,1)S(1)} %pad_maximum_fusion) | copy-start | bytes 1572868
  11.5 3.3 %copy-start.2 = (f32[1024,1]{1,0:T(8,128)}, f32[1024,1]{1,0:T(8,128)S(1)}, u32[]{:S(2)}) copy-start(f32[1024,1]{1,0:T(8,128)S(1)} %select_n.90.rowpoint_ref) | copy-start | bytes 12292
  141.4 75.5 %copy-start.4 = (f32[1024,256]{1,0:T(8,128)S(1)}, f32[1024,256]{1,0:T(8,128)}, u32[]{:S(2)}) copy-start(f32[1024,256]{1,0:T(8,128)} %get-tuple-element.7) | copy-start | bytes 3145732
  216.9 2.0 copy-start.1

commit v3 on v2

--- a/solution.py
+++ b/solution.py
@@ -486,6 +486,387 @@
     )(terms)
 
 
+def fused_kernel(
+    depth, head_dim, x_ref, pick_ref, qhi_ref, qlo_ref, qraw_ref, cot_ref, cott_ref, bias_ref,
+    colscale_ref, colpoint_ref, out_ref, pull_ref, rowsum_ref,
+    g, terms, from_core, from_side, from_low, from_high, s_ref, d_ref,
+    send_sem, recv_sem, local_sem,
+    core_send, core_recv, side_send, side_recv, up_send, low_recv, down_send, high_recv,
+):
+    quads = x_ref.shape[0]
+    cols = qhi_ref.shape[2]
+    chunks = 2 * depth
+    wide = QUAD * HEAD_COLS
+    me, a, b, c = place()
+    side = me + 2 - 4 * b
+    sibling = me + 1 - 2 * c
+    targets = {UP: me + 4, DOWN: me - 4, SIDE: side, SIBLING: sibling}
+    can = {UP: a < depth - 1, DOWN: a > 0}
+    every_way = (UP, DOWN, SIDE, SIBLING)
+    greet(a, depth, side, sibling, me)
+
+    def send(way, slot, q, own=False):
+        src = x_ref.at[q] if own else g.at[q, slot]
+        return remote(
+            src, g.at[q, slot], send_sem.at[way, slot, q], recv_sem.at[slot, q], targets[way]
+        )
+
+    def act(ways, slot, q, own, fn):
+        for way in ways:
+            if way in can:
+                pl.when(can[way])(lambda way=way: fn(send(way, slot, q, own)))
+            else:
+                fn(send(way, slot, q, own))
+
+    def own_copy(q):
+        return pltpu.make_async_copy(x_ref.at[q], g.at[q, me], local_sem.at[q])
+
+    def gather_own(q):
+        act(every_way, me, q, True, lambda copy: copy.start())
+        own_copy(q).start()
+
+    levels = []
+    for step in range(1, depth + 1):
+        routes = []
+        if step < depth:
+            routes.append((a - step >= 0, me - 4 * step, (UP, SIDE, SIBLING)))
+            routes.append((a + step < depth, me + 4 * step, (DOWN, SIDE, SIBLING)))
+        near = step - 1
+        routes.append((a - near >= 0, side - 4 * near, (SIBLING,)))
+        if near:
+            routes.append((a + near < depth, side + 4 * near, (SIBLING,)))
+        levels.append(routes)
+
+    def gather_level(step, q):
+        for valid, slot, ways in levels[step - 1]:
+            @pl.when(valid)
+            def _(slot=slot, ways=ways):
+                send(SIBLING, slot, q).wait_recv()
+                act(ways, slot, q, False, lambda copy: copy.start())
+
+    def gather_finish(q):
+        def body(i, carry):
+            send(SIBLING, 2 * i + 1 - c, q).wait_recv()
+            return carry
+        lax.fori_loop(0, 2 * depth, body, 0)
+        own_copy(q).wait()
+
+    def gather_settle(q):
+        act(every_way, me, q, True, lambda copy: copy.wait_send())
+        for routes in levels:
+            for valid, slot, ways in routes:
+                @pl.when(valid)
+                def _(slot=slot, ways=ways):
+                    act(ways, slot, q, False, lambda copy: copy.wait_send())
+
+    def core_copy(q, dest):
+        return remote(
+            terms.at[q, 1 - c, dest], from_core.at[q, dest],
+            core_send.at[q, dest], core_recv.at[q, dest], sibling,
+        )
+
+    def side_copy(q, z):
+        return remote(
+            terms.at[q, c, 2 * z + 1 - b], from_side.at[q, z],
+            side_send.at[q, z], side_recv.at[q, z], side,
+        )
+
+    def up_copy(q, z):
+        return remote(
+            terms.at[q, c, 2 * z + b], from_low.at[q, z], up_send.at[q, z], low_recv.at[q, z], me + 4
+        )
+
+    def down_copy(q, z):
+        return remote(
+            terms.at[q, c, 2 * z + b], from_high.at[q, z],
+            down_send.at[q, z], high_recv.at[q, z], me - 4,
+        )
+
+    def at_step(step, fn):
+        if step == 0:
+            fn(a, 0)
+        else:
+            pl.when(a + step < depth)(lambda: fn(a + step, 1))
+            pl.when(a - step >= 0)(lambda: fn(a - step, -1))
+
+    def every(fn):
+        for step in range(depth - 1, -1, -1):
+            at_step(step, fn)
+
+    def sum_begin(q):
+        def go(z, _):
+            core_copy(q, 2 * z + 1 - b).start()
+            core_copy(q, 2 * z + b).start()
+        every(go)
+
+    def sum_across(q):
+        def go(z, _):
+            dest = 2 * z + 1 - b
+            core_copy(q, dest).wait_recv()
+            total = terms[q, c, dest].astype(F32) + from_core[q, dest].astype(F32)
+            terms[q, c, dest] = total.astype(BF16)
+            side_copy(q, z).start()
+        every(go)
+
+    def sum_along(step, q):
+        def go(z, way):
+            dest = 2 * z + b
+            core_copy(q, dest).wait_recv()
+            side_copy(q, z).wait_recv()
+
+            def total():
+                part = terms[q, c, dest].astype(F32) + from_core[q, dest].astype(F32)
+                return part + from_side[q, z].astype(F32)
+
+            def put(value):
+                terms[q, c, dest] = value.astype(BF16)
+
+            def below():
+                up_copy(q, z).wait_recv()
+                return from_low[q, z].astype(F32)
+
+            def above():
+                down_copy(q, z).wait_recv()
+                return from_high[q, z].astype(F32)
+
+            if way == 1:
+                pl.when(a > 0)(lambda: put(total() + below()))
+                pl.when(a == 0)(lambda: put(total()))
+                up_copy(q, z).start()
+            elif way == -1:
+                pl.when(a < depth - 1)(lambda: put(total() + above()))
+                pl.when(a == depth - 1)(lambda: put(total()))
+                down_copy(q, z).start()
+            else:
+                out_ref[q] = total()
+
+                @pl.when(a > 0)
+                def _():
+                    out_ref[q] += below()
+
+                @pl.when(a < depth - 1)
+                def _():
+                    out_ref[q] += above()
+        at_step(step, go)
+
+    def sum_settle(q):
+        def go(z, way):
+            core_copy(q, 2 * z + 1 - b).wait_send()
+            core_copy(q, 2 * z + b).wait_send()
+            side_copy(q, z).wait_send()
+            if way == 1:
+                up_copy(q, z).wait_send()
+            elif way == -1:
+                down_copy(q, z).wait_send()
+        every(go)
+
+    zeros = jnp.zeros((HEAD_COLS, cols), BF16)
+    zero8 = tuple(jnp.zeros((8, cols), F32) for _ in range(QUAD))
+    lane = lax.broadcasted_iota(jnp.int32, (cols, 128), 1)
+    half = lax.broadcasted_iota(jnp.int32, (CHUNK, 128), 1) < HEAD_COLS
+
+    def quad_step(q, carry0):
+        ahead = lambda fn: pl.when(q + 1 < quads)(fn)
+        behind = lambda fn: pl.when(q > 0)(fn)
+
+        def load(i, span):
+            parts = []
+            for j in range(2):
+                o = 2 * i + j
+                w = jnp.broadcast_to(pick_ref[pl.ds(o, 1), :], (BLOCK, 128)).astype(BF16)
+                low, high = g[q, o, :BLOCK, span], g[q, o, BLOCK:, span]
+                parts.append(low * (1 - w) + high * w)
+            return jnp.concatenate(parts, axis=0)
+
+        def store(i, span, value):
+            for j in range(2):
+                w = jnp.broadcast_to(pick_ref[pl.ds(2 * i + j, 1), :], (BLOCK, 128))
+                part = value[j * BLOCK : (j + 1) * BLOCK]
+                terms[q, j, i, :BLOCK, span] = (part * (1.0 - w)).astype(BF16)
+                terms[q, j, i, BLOCK:, span] = (part * w).astype(BF16)
+
+        def score_weights(h):
+            rows = slice(h * HEAD_COLS, (h + 1) * HEAD_COLS)
+            hi, lo = qhi_ref[q, rows, :], qlo_ref[q, rows, :]
+            parts = [hi, zeros, lo, zeros] if h % 2 == 0 else [zeros, hi, zeros, lo]
+            return jnp.concatenate(parts, axis=0)
+
+        def cot_weights(h):
+            row = lax.broadcasted_iota(jnp.int32, (QUAD * head_dim, cols), 0)
+            keep = (row >= h * head_dim) & (row < (h + 1) * head_dim)
+            return jnp.where(keep, cott_ref[q], jnp.zeros((), BF16))
+
+        behind(lambda: sum_begin(q - 1))
+        ahead(lambda: gather_level(1, q + 1))
+        qw = [score_weights(h) for h in range(QUAD)]
+        ow = [cot_weights(h) for h in range(QUAD)]
+
+        def scores(i, highest):
+            rows = pl.ds(pl.multiple_of(i * CHUNK, CHUNK), CHUNK)
+            low = bias_ref[pl.ds(i * 2, 1), :]
+            high = bias_ref[pl.ds(i * 2 + 1, 1), :]
+            vals = load(i, slice(wide, wide + 128))
+            pairs = [load(i, slice(n * 128, (n + 1) * 128)) for n in range(QUAD // 2)]
+            out = []
+            for h in range(QUAD):
+                pair = pairs[h // 2]
+                s = dot(jnp.concatenate([pair, pair], axis=1), qw[h])
+                s = jnp.concatenate([s[:BLOCK] + low, s[BLOCK:] + high], axis=0)
+                s_ref[h, rows, :] = s
+                out.append(jnp.maximum(highest[h], fold(s, jnp.max)))
+                d_ref[h, rows, :] = dot(vals, ow[h])
+            return tuple(out)
+
+        highest = lax.fori_loop(
+            0, chunks, scores, tuple(jnp.full((8, cols), -jnp.inf, F32) for _ in range(QUAD))
+        )
+        highest = [jnp.max(x, axis=0, keepdims=True) for x in highest]
+        behind(lambda: sum_across(q - 1))
+        ahead(lambda: gather_level(2, q + 1))
+
+        def exps(i, total):
+            rows = pl.ds(pl.multiple_of(i * CHUNK, CHUNK), CHUNK)
+            out = []
+            for h in range(QUAD):
+                e = jnp.exp(s_ref[h, rows, :] - highest[h])
+                s_ref[h, rows, :] = e
+                out.append(total[h] + fold(e, jnp.sum))
+            return tuple(out)
+
+        total = lax.fori_loop(0, chunks, exps, zero8)
+        inverse = [1.0 / jnp.sum(x, axis=0, keepdims=True) for x in total]
+        ahead(lambda: gather_level(3, q + 1))
+        pl.when(q + 2 < quads)(lambda: gather_own(q + 2))
+        behind(lambda: sum_along(depth - 1, q - 1))
+
+        def deltas(i, delta):
+            rows = pl.ds(pl.multiple_of(i * CHUNK, CHUNK), CHUNK)
+            out = []
+            for h in range(QUAD):
+                p = s_ref[h, rows, :] * inverse[h]
+                low = p.astype(BF16).astype(F32)
+                out.append(delta[h] + fold(low * d_ref[h, rows, :], jnp.sum))
+            return tuple(out)
+
+        delta = lax.fori_loop(0, chunks, deltas, zero8)
+        delta = [jnp.sum(x, axis=0, keepdims=True) for x in delta]
+        for step in range(4, depth + 1):
+            ahead(lambda step=step: gather_level(step, q + 1))
+        behind(lambda: sum_along(depth - 2, q - 1))
+
+        qk = []
+        ok = []
+        for h in range(QUAD):
+            pair = qraw_ref[q, :, (h // 2) * 128 : (h // 2 + 1) * 128]
+            qk.append(jnp.where(lane // HEAD_COLS == h % 2, pair, jnp.zeros((), BF16)))
+            ok.append(jnp.where(lane // head_dim == h, cot_ref[q], jnp.zeros((), BF16)))
+
+        def grads(i, carry):
+            row_total, pulls = carry
+            rows = pl.ds(pl.multiple_of(i * CHUNK, CHUNK), CHUNK)
+            new_total, new_pulls = [], []
+            vterm = None
+            for n in range(QUAD // 2):
+                span = slice(n * 128, (n + 1) * 128)
+                pair = load(i, span)
+                kterm = None
+                col_totals = []
+                for h in (2 * n, 2 * n + 1):
+                    p = s_ref[h, rows, :] * inverse[h]
+                    p_low = p.astype(BF16)
+                    ds = p * (d_ref[h, rows, :] - delta[h])
+                    ds_low = ds.astype(BF16)
+                    new_total.append(row_total[h] + fold(ds, jnp.sum))
+                    col_totals.append(jnp.sum(ds, axis=1, keepdims=True))
+                    kt = dot(ds_low, qk[h])
+                    kterm = kt if kterm is None else kterm + kt
+                    vt = dot(p_low, ok[h])
+                    vterm = vt if vterm is None else vterm + vt
+                    pull = lax.dot_general(
+                        pair, ds_low, (((0,), (0,)), ((), ())), preferred_element_type=F32
+                    )
+                    off = (h % 2) * HEAD_COLS
+                    new_pulls.append(pulls[h] + pull[off : off + HEAD_COLS])
+                sums = jnp.where(half, col_totals[0], col_totals[1])
+                kterm = (
+                    colscale_ref[q, :, span] * kterm
+                    - colpoint_ref[q, :, span] * sums * pair.astype(F32)
+                )
+                store(i, span, kterm)
+            store(i, slice(wide, wide + 128), vterm)
+            return tuple(new_total), tuple(new_pulls)
+
+        pull0 = tuple(jnp.zeros((HEAD_COLS, cols), F32) for _ in range(QUAD))
+        row_total, pulls = lax.fori_loop(0, chunks, grads, (zero8, pull0))
+        for h in range(QUAD):
+            pull_ref[q, h * HEAD_COLS : (h + 1) * HEAD_COLS, :] = pulls[h]
+            rowsum_ref[q, h * 8 : (h + 1) * 8, :] = row_total[h]
+        for step in range(depth - 3, -1, -1):
+            behind(lambda step=step: sum_along(step, q - 1))
+        ahead(lambda: gather_finish(q + 1))
+        return carry0
+
+    gather_own(0)
+    gather_own(1)
+    for step in range(1, depth + 1):
+        gather_level(step, 0)
+    gather_finish(0)
+    lax.fori_loop(0, quads, quad_step, 0)
+    last = quads - 1
+    sum_begin(last)
+    sum_across(last)
+    for step in range(depth - 1, -1, -1):
+        sum_along(step, last)
+
+    def settle(q, carry):
+        gather_settle(q)
+        sum_settle(q)
+        return carry
+
+    lax.fori_loop(0, quads, settle, 0)
+
+
+def fused(packed, owners, pick, qhi, qlo, qraw, cot, cott, bias, vecs, head_dim):
+    quads, rows, features = packed.shape
+    depth = owners // 4
+    cols = qhi.shape[1]
+    kw, vw = QUAD * HEAD_COLS, QUAD * head_dim
+    by_cols = lambda x, width: x.reshape(x.shape[0], quads, width).transpose(1, 0, 2)
+    by_rows = lambda x, height: x.reshape(quads, height, x.shape[1])
+    tile = (rows, features)
+    dma = pltpu.SemaphoreType.DMA
+    vmem = pl.BlockSpec(memory_space=pltpu.VMEM)
+    weights = jnp.broadcast_to(pick.astype(F32)[:, None], (owners, 128))
+    return pl.pallas_call(
+        functools.partial(fused_kernel, depth, head_dim),
+        in_specs=[pl.BlockSpec(memory_space=pl.ANY)] + [vmem] * 9,
+        out_specs=[vmem] * 3,
+        out_shape=[
+            jax.ShapeDtypeStruct((quads,) + tile, F32),
+            jax.ShapeDtypeStruct((quads, kw, cols), F32),
+            jax.ShapeDtypeStruct((quads, QUAD * 8, cols), F32),
+        ],
+        scratch_shapes=[
+            pltpu.VMEM((quads, owners) + tile, BF16),
+            pltpu.VMEM((quads, 2, 2 * depth) + tile, BF16),
+            pltpu.VMEM((quads, 2 * depth) + tile, BF16),
+            pltpu.VMEM((quads, depth) + tile, BF16),
+            pltpu.VMEM((quads, depth) + tile, BF16),
+            pltpu.VMEM((quads, depth) + tile, BF16),
+            pltpu.VMEM((QUAD, owners * BLOCK, cols), F32),
+            pltpu.VMEM((QUAD, owners * BLOCK, cols), F32),
+            dma((4, owners, quads)), dma((owners, quads)), dma((quads,)),
+        ]
+        + [dma((quads, 2 * depth))] * 2
+        + [dma((quads, depth))] * 6,
+        compiler_params=pltpu.CompilerParams(
+            collective_id=2, has_side_effects=True, vmem_limit_bytes=63 * 1024 * 1024
+        ),
+        name="fused_attention",
+    )(packed, weights, by_rows(qhi, kw), by_rows(qlo, kw), by_cols(qraw, kw), by_cols(cot, vw),
+      by_rows(cott, vw), bias, by_cols(vecs[0], kw), by_cols(vecs[1], kw))
+
+
 def split2(x):
     hi = lax.reduce_precision(x, 8, 7)
     return hi.astype(BF16), (x - hi).astype(BF16)
@@ -560,11 +941,23 @@
     quads = heads // QUAD
     by_quad = [kx.reshape(rows, quads, -1), values.reshape(rows, quads, -1)]
     packed = jnp.concatenate(by_quad, axis=2).transpose(1, 0, 2)
-    gathered = gather(packed, owners)
-    terms, qgrad = attention(
-        gathered, fetch_block[0], qhi, qlo, qraw, out_grad, cott, qt, bias, vecs, head_dim
-    )
-    summed = scatter_sum(terms).transpose(1, 0, 2)
+    if owners <= 16:
+        sums, pulls, row_totals = fused(
+            packed, owners, fetch_block[0], qhi, qlo, qraw, out_grad, cott, bias, vecs, head_dim
+        )
+        summed = sums.transpose(1, 0, 2)
+        row_total = jnp.sum(row_totals.reshape(heads, 1, 8, rows), axis=2)
+        row_total = jnp.broadcast_to(row_total, (heads, HEAD_COLS, rows)).reshape(-1, rows)
+        qgrad = (
+            vecs[0].reshape(-1, 1) * pulls.reshape(-1, rows)
+            - vecs[1].reshape(-1, 1) * row_total * qt.astype(F32)
+        )
+    else:
+        gathered = gather(packed, owners)
+        terms, qgrad = attention(
+            gathered, fetch_block[0], qhi, qlo, qraw, out_grad, cott, qt, bias, vecs, head_dim
+        )
+        summed = scatter_sum(terms).transpose(1, 0, 2)
     query_grad, query_point_grad = unlayout(qgrad.T, heads, head_dim, count)
     split = QUAD * HEAD_COLS
     key_grad, key_point_grad = unlayout(summed[:, :, :split], heads, head_dim, count)

time: 223 us -> 234 us (1.049)
  Pallas kernels: 202 us -> 207 us
  local copies, waits for them, and re-layouts: 13.1 us -> 16.3 us
    pallas_call x3 -> x1, Pallas kernels: 202 us -> 207 us  [fused(): pl.pallas_call(functools.partial(fused_kernel, depth, head_dim), in_specs...]
    unnamed x30 -> x20, local copies, waits for them, and re-layouts: 9 us -> 8.28 us
where the time goes in v3:
time: 234 us; the launch traced here: 233 us
  Pallas kernels  207 us (88%)
  local copies, waits for them, and re-layouts  16.3 us (7%)
  other arithmetic  8.55 us (4%)
    pallas_call x1, Pallas kernels, fused(): pl.pallas_call(functools.partial(fused_kernel, depth, head_dim), in_specs...  207 us
    unnamed x20, local copies, waits for them, and re-layouts  8.28 us

profile of v3, /device:TPU:0, one launch (start us, length us, event | category | flops | bytes accessed | tf_op | source)
XLA Modules:
  0.0 233.2 jit_solution(12029124244465480303)
XLA Ops:
  0.9 0.7 convert_bitcast_fusion.1
  1.5 0.7 broadcast_compare_fusion
  2.2 0.8 fusion.7
  3.1 0.7 broadcast_multiply_fusion.1
  4.1 0.6 broadcast_select_fusion.1
  4.8 0.7 broadcast_in_dim.97.pick_ref
  5.5 0.6 copy.102
  6.3 1.1 copy.70
  7.5 1.1 copy.80
  8.6 0.1 copy.79
  8.8 0.2 pad_maximum_fusion
  9.0 0.1 copy.69
  9.3 0.2 copy.78
  9.6 0.8 copy.85
  10.5 0.8 copy.84
  11.6 0.3 concatenate.10
  11.8 0.2 copy.77
  12.0 1.0 maximum_bitcast_fusion.x_ref
  13.0 1.0 copy.82
  14.0 1.3 fusion
  15.3 207.4 %fused_attention.1 = (f32[4,256,384]{2,1,0:T(8,128)}, f32[4,256,256]{2,1,0:T(8,128)}, f32[4,32,256]{2,1,0:T(8,128)}) custom-call(bf16[4,256,384]{2,1,0:T(8,128)(2,1)} %maximum_bitcast_fusion.x_ref, f32[16,128]{1,0:T(8,128)} %broadcast_in_dim.97.pick_ref, bf16[4,256,256]{2,1,0:T(8,128)(2,1)} %bitcast.94, bf16[4,256,256]{2,1,0:T(8,128)(2,1)} %bitcast.93, ...), custom_call_target="tpu_custom_call" | custom-call | tf_op jit(solution)/shard_map/fused_attention/pallas_call | solution.py:840
  222.7 0.9 reduce_sum.22
  223.7 1.6 fusion.4
  225.3 1.0 copy.91
  226.3 0.9 copy.92
  227.3 1.1 slice.29
  228.3 1.3 slice.26
  229.6 0.3 copy.88
  230.0 0.2 copy.90
  230.2 1.0 copy.95
  231.3 1.0 copy.93
  232.3 0.9 copy.94
  (46 shorter events, 1.7 us)
Async XLA Ops:
  0.6 8.0 %copy-start.1 = (bf16[256,512]{1,0:T(8,128)(2,1)S(1)}, bf16[256,512]{1,0:T(8,128)(2,1)}, u32[]{:S(2)}) copy-start(bf16[256,512]{1,0:T(8,128)(2,1)} %param.10) | copy-start | bytes 786436
  6.3 2.7 %copy-start.2 = (bf16[256,512]{1,0:T(8,128)(2,1)S(1)}, bf16[256,512]{1,0:T(8,128)(2,1)}, u32[]{:S(2)}) copy-start(bf16[256,512]{1,0:T(8,128)(2,1)} %param.12) | copy-start | bytes 786436
  7.5 1.7 copy-start.3
  8.6 1.0 copy-start
